TPU v7x, 256 devices: a whole 4x4x8 slice. The times are simulated.
256 devices in a mesh: role: 4 (over x_lo, core), fsdp: 64 (over y, x_hi, z).
Axes of the slice: x: 4 (x_hi: 2, x_lo: 2; x = x_hi * 2 + x_lo), y: 4, z: 8, core: 2. Of those that a mesh axis runs over, the one named last changes fastest.
Arguments:
- source_noise: bfloat16 [24576, 64], P('fsdp'), may hold values from -6 to 6
- score_noise: bfloat16 [24576, 64], P('fsdp'), may hold values from -6 to 6
- noise_level: float32 [24576], P('fsdp'), may hold values from 0.05 to 0.95
- embed_weight: bfloat16 [4, 64, 3072], P('role'), may hold values from -0.75 to 0.75
- time_vector: float32 [4, 3072], P('role'), may hold values from -6 to 6
- norm_gain: float32 [4, 3072], P('role'), may hold values from 0.5 to 1.5
- block_weight: bfloat16 [4, 3072, 1536], P('role', 'fsdp'), may hold values from -0.109375 to 0.109375
- readout_weight: bfloat16 [4, 1536, 64], P('role'), may hold values from -0.15625 to 0.15625
Outputs:
- grads: float32 [4, 3072, 1536], P('role', 'fsdp')
- generated: bfloat16 [24576, 64], P('fsdp')
All inputs are finite; a program needn't handle non-finite values. Where the computation divides by a largest or mean magnitude, that divisor is 1e-20 or more.
Results may differ from a plain program's by a relative error of at most 0.0065.
Values may be sent and summed in bfloat16 or wider, within the bound.
A program may use at most 128 MiB of HBM per device.

v0:
```python
import math

import jax
import jax.numpy as jnp
from jax import lax
from jax.sharding import PartitionSpec as P

adv_weight = 3.0


def broadcast(value, axis, root):
    mine = lax.axis_index(axis) == root
    return lax.psum(jnp.where(mine, value, jnp.zeros_like(value)), axis)


def norm_rows(preact, gain_row):
    return preact * lax.rsqrt(jnp.mean(preact * preact, axis=-1, keepdims=True) + 1e-06) * gain_row


def score_net(latent, level, embed_w, time_w, gain_row, block_w, readout_w):
    preact = (
        jnp.dot(latent, embed_w, preferred_element_type=jnp.float32)
        + level[:, None] * time_w[None, :]
    )
    normed = norm_rows(preact, gain_row).astype(jnp.bfloat16)
    hidden = jnp.dot(normed, block_w, preferred_element_type=jnp.float32)
    activated = jax.nn.gelu(hidden, approximate=True).astype(jnp.bfloat16)
    output = jnp.dot(activated, readout_w, preferred_element_type=jnp.float32).astype(jnp.bfloat16)
    return (preact, normed, hidden, output)


def hidden_grad(hidden, cotangent, readout_w):
    back = jnp.dot(cotangent, readout_w.astype(jnp.float32).T, precision=lax.Precision.HIGHEST)
    unused, gelu_back = jax.vjp(lambda value: jax.nn.gelu(value, approximate=True), hidden)
    return gelu_back(back)[0].astype(jnp.bfloat16)


def input_grad(hcot, preact, gain_row, block_w, embed_w):
    normed_back = lax.dot_general(
        hcot, block_w, (((1,), (1,)), ((), ())), preferred_element_type=jnp.float32
    )
    unused, norm_back = jax.vjp(lambda value: norm_rows(value, gain_row), preact)
    pre_back = norm_back(normed_back)[0]
    return jnp.dot(pre_back, embed_w.astype(jnp.float32).T, precision=lax.Precision.HIGHEST)


def shards(
    source_noise,
    score_noise,
    noise_level,
    embed_weight,
    time_vector,
    norm_gain,
    block_weight,
    readout_weight,
):
    group_index = lax.axis_index("role")
    embed_w = embed_weight[0]
    time_w = time_vector[0]
    gain_row = norm_gain[0]
    readout_w = readout_weight[0]
    gathered = lax.all_gather(block_weight[0], "fsdp", axis=0, tiled=True)
    ones = jnp.ones_like(noise_level)
    pre_first, normed_first, hidden_first, own_first = score_net(
        source_noise, ones, embed_w, time_w, gain_row, gathered, readout_w
    )
    generated = broadcast(own_first, "role", 0)
    level = noise_level[:, None]
    noised = (
        (1.0 - level) * generated.astype(jnp.float32) + level * score_noise.astype(jnp.float32)
    ).astype(jnp.bfloat16)
    pre_second, normed_second, hidden_second, scores = score_net(
        noised, noise_level, embed_w, time_w, gain_row, gathered, readout_w
    )
    gen32 = generated.astype(jnp.float32)
    score32 = scores.astype(jnp.float32)
    logit = jnp.sum(score32, axis=-1, keepdims=True)
    adv_cot = jnp.broadcast_to(-jax.nn.sigmoid(-logit), scores.shape)
    adv_hcot = hidden_grad(hidden_second, adv_cot, readout_w)
    latent_back = input_grad(adv_hcot, pre_second, gain_row, gathered, embed_w)
    adversarial = (adv_weight * (1.0 - level) * latent_back).astype(jnp.bfloat16)
    empty_rows = jnp.zeros_like(scores)
    is_score = (group_index == 1) | (group_index == 2)
    piece = jnp.where(is_score, scores, jnp.where(group_index == 3, adversarial, empty_rows))
    collected = lax.all_gather(piece[None], "role", axis=0, tiled=True)
    real32 = collected[1].astype(jnp.float32)
    fake32 = collected[2].astype(jnp.float32)
    spread = jnp.mean(jnp.abs(gen32 - real32), axis=-1, keepdims=True) + 1e-05
    dmd = ((fake32 - real32) / spread).astype(jnp.bfloat16)
    push = dmd.astype(jnp.float32) + collected[3].astype(jnp.float32)
    critic_cot = jnp.broadcast_to(jax.nn.sigmoid(logit), scores.shape)
    zero_cot = jnp.zeros_like(push)
    cotangent = jnp.where(
        group_index == 0,
        push,
        jnp.where(
            group_index == 2, score32 - gen32, jnp.where(group_index == 3, critic_cot, zero_cot)
        ),
    )
    chosen_normed = jnp.where(group_index == 0, normed_first, normed_second)
    chosen_hidden = jnp.where(group_index == 0, hidden_first, hidden_second)
    hcot = hidden_grad(chosen_hidden, cotangent, readout_w)
    factor = 1.0 / math.sqrt(source_noise.shape[0] * lax.axis_size("fsdp"))
    partial_grad = lax.psum_scatter(
        lax.dot_general(
            chosen_normed, hcot, (((0,), (0,)), ((), ())), preferred_element_type=jnp.float32
        )
        * factor,
        "fsdp",
        scatter_dimension=0,
        tiled=True,
    )
    return (partial_grad[None], generated)


def solution(mesh):
    in_specs = (
        P("fsdp", None),
        P("fsdp", None),
        P("fsdp"),
        P("role", None, None),
        P("role", None),
        P("role", None),
        P("role", "fsdp", None),
        P("role", None, None),
    )
    out_specs = (P("role", "fsdp", None), P("fsdp", None))
    return jax.shard_map(shards, mesh=mesh, in_specs=in_specs, out_specs=out_specs, check_vma=False)
```

profile of v0, /device:TPU:2, one launch (start us, length us, event | category | flops | bytes accessed | tf_op | source)
XLA Modules:
  0.0 1110.8 jit_solution(13597602335349028306)
XLA Ops:
  7.2 0.0 copy-start
  7.2 0.0 all-gather.4.cloned.1.call-start
  7.2 0.7 all-gather.4.cloned.1.call-update
  7.9 0.0 reduce-scatter.2.cloned.1.call-start
  8.0 0.2 copy-done
  8.2 3.9 multiply_reduce_fusion.2
  12.1 158.5 %all-gather.4.cloned.1.call-done = bf16[1,3072,1536]{2,1,0:T(8,128)(2,1)} async-done(((bf16[1,48,1536]{2,1,0:T(8,128)(2,1)}), bf16[1,3072,1536]{2,1,0:T(8,128)(2,1)}) %all-gather.4.cloned.1.call-update) | async-done | bytes 9437200 | tf_op jit(solution)/shard_map/all_gather | solution.py:62
  170.6 7.9 fusion.4
  178.5 0.0 copy-start.2
  178.5 0.0 copy-start.4
  178.5 0.9 fusion.47
  179.5 10.7 psum.7
  190.2 0.0 copy-start.1
  190.2 1.0 multiply_reduce_fusion.1
  191.2 6.6 fusion.2
  197.8 0.9 convert_reduce_fusion
  198.8 2.8 fusion.18
  201.6 6.6 multiply_reduce_fusion
  208.3 3.2 fusion.51
  211.5 5.8 all-gather.1
  217.4 2.7 fusion.25
  220.1 9.6 convolution_multiply_fusion
  229.8 0.0 reduce-scatter.2.cloned.1.call-update
  229.8 874.2 %reduce-scatter.2.cloned.1.call-done = f32[48,1536]{1,0:T(8,128)} async-done(((f32[3072,1536]{1,0:T(8,128)}), f32[48,1536]{1,0:T(8,128)}) %reduce-scatter.2.cloned.1.call-update) | async-done | bytes 294928 | tf_op jit(solution)/shard_map/reduce_scatter | solution.py:104
  (21 shorter events, 0.1 us)
Async XLA Ops:
  7.2 1.0 copy-start
  7.2 163.4 %all-gather.4.cloned.1.call-start = ((), (), s32[]{:S(2)}) async-start(), calls=%async_computation.2 | async-start | bytes 9584640 | tf_op jit(solution)/shard_map/all_gather | solution.py:62
  7.9 1096.1 %reduce-scatter.2.cloned.1.call-start = ((), (), s32[]{:S(2)}) async-start(), calls=%async_computation.1 | async-start | bytes 19169280 | tf_op jit(solution)/shard_map/reduce_scatter | solution.py:104
  8.2 3.9 copy-start.5
  8.2 162.4 %copy-start.3 = (f32[1,3072]{1,0:T(1,128)S(1)}, f32[1,3072]{1,0:T(1,128)}, u32[]{:S(2)}) copy-start(f32[1,3072]{1,0:T(1,128)} %param.13) | copy-start | bytes 36868
  170.6 7.9 copy-start.6
  178.5 11.7 %copy-start.2 = (bf16[384,64]{0,1:T(8,128)(2,1)S(1)}, bf16[384,64]{0,1:T(8,128)(2,1)}, u32[]{:S(2)}) copy-start(bf16[384,64]{0,1:T(8,128)(2,1)} %param.9) | copy-start | bytes 147460
  178.5 11.7 %copy-start.4 = (f32[1,3072]{1,0:T(1,128)S(1)}, f32[1,3072]{1,0:T(1,128)}, u32[]{:S(2)}) copy-start(f32[1,3072]{1,0:T(1,128)} %param.12) | copy-start | bytes 36868
  190.2 27.2 %copy-start.1 = (bf16[384,64]{0,1:T(8,128)(2,1)}, bf16[384,64]{0,1:T(8,128)(2,1)S(1)}, u32[]{:S(2)}) copy-start(bf16[384,64]{0,1:T(8,128)(2,1)S(1)} %psum.7) | copy-start | bytes 147460
  208.2 11.9 %slice-start = ((s8[4718592]{0:T(1024)(128)(4,1)}), s8[4194304]{0:T(1024)(128)(4,1)S(1)}, s32[]{:S(2)}) async-start(s8[4718592]{0:T(1024)(128)(4,1)} %bitcast.39), calls=%async_computation.3 | async-start | bytes 8388608
  217.4 2.7 slice-start.1
Sparse Core Ops, SparseCore 0:
  11.7 158.8 all-gather.3
  229.9 874.0 reduce-scatter.1
where the time goes:
time: 1110 us
  waiting for transfers between devices  1030 us (93%)
  matrix products  46.3 us (4%)
  blocking collectives  16.5 us (1%)
  between operations  14.2 us (1%)
    reduce_scatter x1, waiting for transfers between devices, shards(): lax.psum_scatter(lax.dot_general(chosen_normed, hcot, (((0,), (0,)), ((),...  874 us
    all_gather x1, waiting for transfers between devices, shards(): gathered = lax.all_gather(block_weight[0], 'fsdp', axis=0, tiled=True)  159 us
  transfers between devices with their start and end apart: 2, of which 2 were waited for; matrix products, arithmetic and copies ran while one was open for 0% of the time, Pallas kernels for 0%

commit v1 on v0

v1 whole, which is shorter than its diff:
```python
import math

import jax
import jax.numpy as jnp
from jax import lax
from jax.sharding import PartitionSpec as P

adv_weight = 3.0
HIGH = lax.Precision.HIGHEST


def forward(latent, level, lifted, folded, readout_w):
    rows = jnp.concatenate([latent.astype(jnp.float32), level[:, None]], axis=1)
    preact = jnp.dot(rows, lifted, precision=HIGH)
    inverse = lax.rsqrt(jnp.mean(preact * preact, axis=-1, keepdims=True) + 1e-06)
    hidden = inverse * jnp.dot(rows, folded, precision=HIGH)
    activated = jax.nn.gelu(hidden, approximate=True).astype(jnp.bfloat16)
    output = jnp.dot(activated, readout_w, preferred_element_type=jnp.float32).astype(jnp.bfloat16)
    return rows, preact, inverse, hidden, output


def hidden_grad(hidden, cotangent, readout_w):
    back = jnp.dot(cotangent, readout_w.astype(jnp.float32).T, precision=HIGH)
    unused, gelu_back = jax.vjp(lambda value: jax.nn.gelu(value, approximate=True), hidden)
    return gelu_back(back)[0]


def shards(
    source_noise,
    score_noise,
    noise_level,
    embed_weight,
    time_vector,
    norm_gain,
    block_weight,
    readout_weight,
):
    role = lax.axis_index("role")
    place = lax.axis_index("fsdp")
    block_w = block_weight[0]
    depth = block_w.shape[0]
    readout_w = readout_weight[0]
    lifted = jnp.concatenate([embed_weight[0].astype(jnp.float32), time_vector], axis=0)
    own = lax.dynamic_slice_in_dim(lifted * norm_gain, place * depth, depth, axis=1)
    folded = lax.psum(jnp.dot(own, block_w.astype(jnp.float32), precision=HIGH), "fsdp")
    ones = jnp.ones_like(noise_level)
    rows0, pre0, inverse0, hidden0, first = forward(source_noise, ones, lifted, folded, readout_w)
    generated = lax.all_gather(first[None], "role", axis=0, tiled=True)[0]
    gen32 = generated.astype(jnp.float32)
    level = noise_level[:, None]
    noised = ((1.0 - level) * gen32 + level * score_noise.astype(jnp.float32)).astype(jnp.bfloat16)
    rows1, pre1, inverse1, hidden1, scores = forward(
        noised, noise_level, lifted, folded, readout_w
    )
    score32 = scores.astype(jnp.float32)
    logit = jnp.sum(score32, axis=-1, keepdims=True)
    adv_cot = jnp.broadcast_to(-jax.nn.sigmoid(-logit), scores.shape)
    adv_hcot = hidden_grad(hidden1, adv_cot, readout_w).astype(jnp.bfloat16).astype(jnp.float32)
    through = jnp.dot(adv_hcot, folded.T, precision=HIGH)
    pulled = jnp.sum(through * rows1, axis=-1, keepdims=True)
    lift_back = jnp.dot(pre1, lifted[:-1].T, precision=HIGH)
    latent_back = inverse1 * through[:, :-1] - (
        inverse1 * inverse1 * inverse1 / lifted.shape[1] * pulled * lift_back
    )
    adversarial = (adv_weight * (1.0 - level) * latent_back).astype(jnp.bfloat16)
    piece = jnp.where(role == 3, adversarial, scores)
    collected = lax.all_gather(piece[None], "role", axis=0, tiled=True)
    real32 = collected[1].astype(jnp.float32)
    fake32 = collected[2].astype(jnp.float32)
    spread = jnp.mean(jnp.abs(gen32 - real32), axis=-1, keepdims=True) + 1e-05
    dmd = ((fake32 - real32) / spread).astype(jnp.bfloat16)
    push = dmd.astype(jnp.float32) + collected[3].astype(jnp.float32)
    critic_cot = jnp.broadcast_to(jax.nn.sigmoid(logit), scores.shape)
    cotangent = jnp.where(
        role == 0,
        push,
        jnp.where(role == 2, score32 - gen32, jnp.where(role == 3, critic_cot, 0.0)),
    )
    rows = jnp.where(role == 0, rows0, rows1)
    inverse = jnp.where(role == 0, inverse0, inverse1)
    hidden = jnp.where(role == 0, hidden0, hidden1)
    hcot = (inverse * hidden_grad(hidden, cotangent, readout_w)).astype(jnp.bfloat16)
    summed = lax.psum(
        lax.dot_general(
            rows, hcot.astype(jnp.float32), (((0,), (0,)), ((), ())), precision=HIGH
        ),
        "fsdp",
    )
    factor = 1.0 / math.sqrt(source_noise.shape[0] * lax.axis_size("fsdp"))
    grad = lax.dot_general(own * factor, summed, (((0,), (0,)), ((), ())), precision=HIGH)
    return (grad[None], generated)


def solution(mesh):
    in_specs = (
        P("fsdp", None),
        P("fsdp", None),
        P("fsdp"),
        P("role", None, None),
        P("role", None),
        P("role", None),
        P("role", "fsdp", None),
        P("role", None, None),
    )
    out_specs = (P("role", "fsdp", None), P("fsdp", None))
    return jax.shard_map(shards, mesh=mesh, in_specs=in_specs, out_specs=out_specs, check_vma=False)
```

time: 1110 us -> 1400 us (1.26)
  waiting for transfers between devices: 1030 us -> 1340 us
  matrix products: 46.3 us -> 27.8 us
    psum x0 -> x2, waiting for transfers between devices: none -> 1340 us  [the longest x1 673 us: shards(): lax.psum(jnp.dot(own, block_w.astype(jnp.float32), precision=HIGH), 'fsdp')]
    reduce_scatter x1 -> x0, waiting for transfers between devices: 874 us -> none  [shards(): lax.psum_scatter(lax.dot_general(chosen_normed, hcot, (((0,), (0,)), ((),...]
    all_gather x1 -> x0, waiting for transfers between devices: 159 us -> none  [shards(): gathered = lax.all_gather(block_weight[0], 'fsdp', axis=0, tiled=True)]
    dot_general x11 -> x13, matrix products: 46.3 us -> 27.8 us  [the longest x2 6.51 us: forward(): preact = jnp.dot(rows, lifted, precision=HIGH)]
where the time goes in v1:
time: 1400 us
  waiting for transfers between devices  1340 us (96%)
  matrix products  27.8 us (2%)
  between operations  14.2 us (1%)
    psum x1, waiting for transfers between devices, shards(): lax.psum(jnp.dot(own, block_w.astype(jnp.float32), precision=HIGH), 'fsdp')  673 us
    psum x1, waiting for transfers between devices, shards(): lax.psum(lax.dot_general(rows, hcot.astype(jnp.float32), (((0,), (0,)), (...  669 us
  transfers between devices with their start and end apart: 2, of which 2 were waited for; matrix products, arithmetic and copies ran while one was open for 0% of the time, Pallas kernels for 0%

profile of v1, /device:TPU:2, one launch (start us, length us, event | category | flops | bytes accessed | tf_op | source)
XLA Modules:
  0.0 1397.3 jit_solution(14437180980682959975)
XLA Ops:
  7.2 0.0 copy-start
  7.2 0.0 all-reduce.4.cloned.1.call-start
  7.3 1.1 bitcast_convert_fusion
  8.3 0.8 dynamic-slice
  9.1 2.1 fusion.41
  11.2 0.0 all-reduce.4.cloned.1.call-update
  11.3 0.0 all-reduce.6.cloned.1.call-start
  11.3 2.3 fusion.23
  13.7 673.0 %all-reduce.4.cloned.1.call-done = f32[65,1536]{1,0:T(8,128)} async-done(((f32[65,1536]{1,0:T(8,128)}), f32[65,1536]{1,0:T(8,128)}) %all-reduce.4.cloned.1.call-update) | async-done | bytes 399376 | tf_op jit(solution)/shard_map/psum | solution.py:45
  686.6 2.1 convolution_multiply_fusion.2
  688.8 0.9 fusion.30
  689.7 5.8 all-gather
  695.5 4.2 multiply_reduce_fusion
  699.8 2.1 convolution_multiply_fusion.1
  701.9 0.9 convert_reduce_fusion
  702.8 2.8 fusion.6
  705.6 1.2 multiply_reduce_fusion.1
  706.8 2.6 fusion.34
  709.4 5.8 all-gather.1
  715.3 2.8 fusion.14
  718.1 1.5 fusion.43
  719.6 0.0 all-reduce.6.cloned.1.call-update
  719.6 668.6 %all-reduce.6.cloned.1.call-done = f32[65,1536]{1,0:T(8,128)} async-done(((f32[65,1536]{1,0:T(8,128)}), f32[65,1536]{1,0:T(8,128)}) %all-reduce.6.cloned.1.call-update) | async-done | bytes 399376 | tf_op jit(solution)/shard_map/psum | solution.py:83
  1388.2 2.3 convolution_bitcast_fusion
  (24 shorter events, 0.2 us)
Async XLA Ops:
  7.2 681.6 %copy-start = (bf16[1,1536,64]{1,2,0:T(8,128)(2,1)S(1)}, bf16[1,1536,64]{1,2,0:T(8,128)(2,1)}, u32[]{:S(2)}) copy-start(bf16[1,1536,64]{1,2,0:T(8,128)(2,1)} %param.15) | copy-start | bytes 589828
  7.2 4.1 copy-start.5
  7.2 4.1 copy-start.3
  7.2 679.4 %all-reduce.4.cloned.1.call-start = ((), (), s32[]{:S(2)}) async-start(), calls=%async_computation | async-start | bytes 884736 | tf_op jit(solution)/shard_map/psum | solution.py:45
  9.1 4.5 copy-start.7
  11.3 1377.0 %all-reduce.6.cloned.1.call-start = ((), (), s32[]{:S(2)}) async-start(), calls=%async_computation.1 | async-start | bytes 884736 | tf_op jit(solution)/shard_map/psum | solution.py:83
  688.8 6.7 copy-start.6
  695.5 19.8 %copy-start.4 = (bf16[384,64]{0,1:T(8,128)(2,1)}, bf16[384,64]{0,1:T(8,128)(2,1)S(1)}, u32[]{:S(2)}) copy-start(bf16[384,64]{0,1:T(8,128)(2,1)S(1)} %get-tuple-element.3) | copy-start | bytes 147460
  695.5 4.2 copy-start.1
  702.8 4.0 copy-start.2
Sparse Core Ops, SparseCore 0:
  11.4 675.2 all-reduce.3
  719.8 668.4 all-reduce.5

commit v2 on v1

v2 whole, which is shorter than its diff:
```python
import functools
import math

import jax
import jax.numpy as jnp
from jax import lax
from jax.experimental import pallas as pl
from jax.experimental.pallas import tpu as pltpu
from jax.sharding import PartitionSpec as P

MESH = pl.DeviceIdType.MESH
f32, bf16 = jnp.float32, jnp.bfloat16
adv_weight = 3.0
ROWS = 384
C = 64
D = 3072
F = 1536
DEPTH = 48
CHUNK = 256
CHUNKS = F // CHUNK
SIDE = 8
HALF = F // 2
ROOT = math.sqrt(2.0 / math.pi)
CUBE = 0.044715 * ROOT


def dot(a, b):
    return jnp.dot(a, b, preferred_element_type=f32)


def dot_nt(a, b):
    return lax.dot_general(a, b, (((1,), (1,)), ((), ())), preferred_element_type=f32)


def split(value):
    high = value.astype(bf16)
    return high, (value - high.astype(f32)).astype(bf16)


def lanes(shape):
    return lax.broadcasted_iota(jnp.int32, shape, len(shape) - 1)


def pack(value):
    top, bottom = value[: ROWS // 2], value[ROWS // 2 :]
    return jnp.where(lanes(top.shape) < C, top, bottom)


def unpack(value):
    turned = pltpu.roll(value, C, 1)
    left = lanes(value.shape) < C
    return jnp.concatenate([jnp.where(left, value, turned), jnp.where(left, turned, value)], axis=0)


def gelu_parts(hidden):
    square = hidden * hidden
    half = 0.5 + 0.5 * jnp.tanh(hidden * (ROOT + CUBE * square))
    return square, half, hidden * half


def gelu_slope(square, half, value):
    return half + value * (1.0 - half) * (2.0 * ROOT + 6.0 * CUBE * square)


def kernel(
    sn, sc, lv, emb, tim, gain, blk, rdo,
    grads, gen_out,
    x_ref, vt, vrow, s_a, d_a, s_b, d_b, m_buf, m_aug,
    t_a, e_a, t_b, e_b, h_buf,
    r2, gram, level, z_f32, z_aug, z_t, rs, y_ref, hid, slope, acc, back_acc, lt, cot,
    gen_pk, gen_in, out_pk, col_in,
    send_m, recv_m, send_h, recv_h, send_g, recv_g, send_c, recv_c,
):
    role = lax.axis_index("role")
    place = lax.axis_index("fsdp")
    p, z = place // SIDE, place % SIDE

    def yx_peer(k):
        return (role, lax.rem(p + k, SIDE) * SIDE + z)

    def z_peer(k):
        return (role, p * SIDE + lax.rem(z + k, SIDE))

    def role_peer(k):
        return (lax.rem(role + k, 4), place)

    barrier = pltpu.get_barrier_semaphore()
    for k in range(1, SIDE):
        pl.semaphore_signal(barrier, inc=1, device_id=yx_peer(k), device_id_type=MESH)
        pl.semaphore_signal(barrier, inc=1, device_id=z_peer(k), device_id_type=MESH)
    for k in range(1, 4):
        pl.semaphore_signal(barrier, inc=1, device_id=role_peer(k), device_id_type=MESH)

    def remote(src, dst, send, recv, device):
        return pltpu.make_async_remote_copy(
            src_ref=src, dst_ref=dst, send_sem=send, recv_sem=recv, device_id=device,
            device_id_type=MESH,
        )

    begin = place * DEPTH
    window = jnp.minimum(begin // 128, D // 128 - 2) * 128
    window = pl.multiple_of(window, 128)
    wide = pl.ds(window, 256)
    gain_w = gain[:, wide]
    lifted = jnp.concatenate(
        [
            emb[0, :, wide].astype(f32) * gain_w,
            jnp.where(
                lax.broadcasted_iota(jnp.int32, (16, 256), 0) == 0, tim[:, wide] * gain_w, 0.0
            ),
        ],
        axis=0,
    )
    lifted = pltpu.roll(lifted, lax.rem(256 + window - begin, 256), 1)[:, :128]
    high, low = split(lifted[:, :DEPTH])
    block = blk[0]
    x_ref[...] = dot(high, block) + dot(low, block)

    def stage_a_fill(send, wide_type):
        vt[...] = jnp.zeros_like(vt)
        for i in range(F // 128):
            vt[i : i + 1, :] = x_ref[C : C + 1, i * 128 : i * 128 + 128]
        tile = vt[...]
        for piece in range(SIDE):
            top, left = piece // 2 * 16, piece % 2 * HALF
            part = x_ref[top : top + 16, left : left + HALF]
            if wide_type:
                send[piece, :, :HALF] = part
                send[piece, :, HALF:] = tile
            else:
                send[piece, :, :HALF] = part.astype(bf16)
                v_high, v_low = split(tile)
                send[piece, :, HALF : HALF + 128] = v_high
                send[piece, :, HALF + 128 :] = v_low

    def stage_a(send, dest, ss, rr):
        return [
            remote(send.at[lax.rem(p + k, SIDE)], dest.at[k], ss.at[0, k], rr.at[0, k], yx_peer(k))
            for k in range(1, SIDE)
        ]

    def stage_b(send, dest, ss, rr):
        return [
            remote(send, dest.at[k], ss.at[1, k], rr.at[1, k], z_peer(k)) for k in range(1, SIDE)
        ]

    own_top = pl.multiple_of(p // 2 * 16, 16)
    own_left = pl.multiple_of(lax.rem(p, 2) * HALF, 128)

    def stage_c(buf, ss, rr):
        own = buf.at[pl.ds(own_top, 16), pl.ds(own_left, HALF)]
        return [remote(own, own, ss.at[2, k], rr.at[2, k], yx_peer(k)) for k in range(1, SIDE)]

    def start(copies):
        for copy in copies:
            copy.start()

    def arrive(copies):
        for copy in copies:
            copy.wait_recv()

    def finish(copies):
        for copy in copies:
            copy.wait_send()

    def total(first, dest):
        value = first.astype(f32)
        for k in range(1, SIDE):
            value = value + dest[k].astype(f32)
        return value

    def put_row(tile):
        vt[...] = tile
        for i in range(F // 128):
            vrow[0:1, i * 128 : i * 128 + 128] = vt[i : i + 1, :]

    stage_a_fill(s_a, True)
    pl.semaphore_wait(barrier, 2 * (SIDE - 1) + 3)
    m_a = stage_a(s_a, d_a, send_m, recv_m)
    start(m_a)

    lt[...] = jnp.concatenate([lifted, jnp.zeros((48, 128), f32)], axis=0).T[:DEPTH]
    for i in range(ROWS // 128):
        level[i * 128 : i * 128 + 128, :] = jnp.broadcast_to(lv[i : i + 1, :], (128, 128)).T
    readout = rdo[0].astype(f32)
    r2[...] = jnp.concatenate([readout, readout], axis=1).astype(bf16)
    time = tim[...]
    t_1 = time.astype(bf16).astype(f32)
    t_2 = (time - t_1).astype(bf16).astype(f32)
    t_3 = time - t_1 - t_2
    rows = lax.broadcasted_iota(jnp.int32, (16, D), 0)
    parts = jnp.where(rows == 0, t_1, jnp.where(rows == 1, t_2, jnp.where(rows == 2, t_3, 0.0)))
    square_e = dot_nt(emb[0], emb[0])
    cross = jnp.sum(dot_nt(parts.astype(bf16), emb[0]), axis=0, keepdims=True)
    square_e = jnp.concatenate([square_e, square_e], axis=1)
    cross = jnp.concatenate([cross, cross], axis=1)
    square_t = jnp.sum(time * time, axis=1, keepdims=True)
    g_1, rest = split(square_e)
    rest = square_e - g_1.astype(f32)
    g_2, g_3 = split(rest)
    gram[0:64, :] = g_1
    gram[64:128, :] = g_2
    gram[128:192, :] = g_3
    gram[192:256, :] = jnp.zeros((64, 128), bf16)

    def rows_in(latent, lev):
        lane = lanes((ROWS, 128))
        lev_high = lev.astype(bf16).astype(f32)
        lev_low = lev - lev_high
        z_f32[...] = latent
        latent16 = latent.astype(bf16)
        z_aug[:, :128] = latent16
        z_aug[:, 128:] = jnp.where(
            lane < 2, lev_high, jnp.where(lane == 2, lev_low, 0.0)
        ).astype(bf16)
        y = (
            dot(latent16, gram[0:128, :]) + dot(latent16, gram[128:256, :]) + lev * cross
        )
        y_ref[...] = y
        mean = (
            0.5 * jnp.sum(latent * (y + lev * cross), axis=1, keepdims=True)
            + lev[:, :1] * lev[:, :1] * square_t
        ) * (1.0 / D)
        rs[...] = jnp.broadcast_to(lax.rsqrt(jnp.maximum(mean, 0.0) + 1e-06), (ROWS, CHUNK))

    def rows_turned():
        lane = lanes((ROWS, 128))
        lev = jnp.where(role == 0, 1.0, level[...])
        lev_high = lev.astype(bf16).astype(f32)
        lev_low = lev - lev_high
        turned = jnp.where(
            lane < C, z_f32[...], jnp.where(lane == C, lev_high, jnp.where(lane == C + 1, lev_low, 0.0))
        ).T
        z_t[...] = turned[:80].astype(bf16)

    arrive(m_a)
    summed = total(s_a[p], d_a)
    s_b[...] = summed
    m_b = stage_b(s_b, d_b, send_m, recv_m)
    start(m_b)
    m_aug[128 + 16 :, :] = jnp.zeros((128 - 16, F), bf16)

    @pl.when(role == 0)
    def _():
        noise = sn[...].astype(f32)
        rows_in(jnp.concatenate([noise, noise], axis=1), jnp.ones((ROWS, 128), f32))

    arrive(m_b)
    summed = total(summed, d_b)
    m_buf[pl.ds(own_top, 16), pl.ds(own_left, HALF)] = summed[:, :HALF]
    m_c = stage_c(m_buf, send_m, recv_m)
    start(m_c)
    put_row(summed[:, HALF:])
    v_full = vrow[0:1, :]
    v_high = v_full.astype(bf16).astype(f32)
    rows = lax.broadcasted_iota(jnp.int32, (16, F), 0)
    m_aug[128:144, :] = jnp.where(
        (rows == 0) | (rows == 2), v_high, jnp.where(rows == 1, v_full - v_high, 0.0)
    ).astype(bf16)
    arrive(m_c)
    high, low = split(m_buf[...])
    m_aug[0:64, :] = high
    m_aug[64:128, :] = low
    finish(m_a)
    finish(m_b)
    finish(m_c)

    def columns(c):
        return pl.ds(pl.multiple_of(c * CHUNK, CHUNK), CHUNK)

    def forward(critic):
        acc[...] = jnp.zeros_like(acc)
        if critic:
            back_acc[...] = jnp.zeros_like(back_acc)

        def body(c, carry):
            cs = columns(c)
            hidden = dot(z_aug[...], m_aug[:, cs]) * rs[...]
            square, half, value = gelu_parts(hidden)
            acc[...] += dot(value.astype(bf16), r2[cs, :])
            if critic:
                rise = gelu_slope(square, half, value)
                slope[:, cs] = rise * rs[...]
                weight = dot_nt(jnp.ones((16, C), bf16), rdo[0, cs, :])[0:1, :]
                back_acc[...] += dot_nt((rise * weight).astype(bf16), m_aug[:, cs])
            else:
                hid[:, cs] = hidden
            return carry

        lax.fori_loop(0, CHUNKS, body, 0)
        return acc[...].astype(bf16).astype(f32)

    def slopes():
        def body(c, carry):
            cs = columns(c)
            slope[:, cs] = gelu_slope(*gelu_parts(hid[:, cs])) * rs[...]
            return carry

        lax.fori_loop(0, CHUNKS, body, 0)

    to_gen = (0, place)

    @pl.when(role == 0)
    def _():
        out = forward(False)
        gen_pk[...] = pack(out).astype(bf16)
        copies = [
            remote(gen_pk, gen_in, send_g.at[k], recv_g.at[0], (k, place)) for k in range(1, 4)
        ]
        start(copies)
        gen_out[...] = out[:, :C].astype(bf16)
        slopes()
        rows_turned()
        finish(copies)
        sources = [
            remote(out_pk, col_in.at[k], send_c.at[0], recv_c.at[k], (k, place))
            for k in range(1, 4)
        ]
        arrive(sources)
        real = unpack(col_in[1].astype(f32))
        fake = unpack(col_in[2].astype(f32))
        adversarial = unpack(col_in[3].astype(f32))
        spread = jnp.sum(jnp.abs(out - real), axis=1, keepdims=True) * (0.5 / C) + 1e-05
        dmd = ((fake - real) / spread).astype(bf16).astype(f32)
        cot[...] = dmd + adversarial

    @pl.when(role != 0)
    def _():
        remote(gen_pk, gen_in, send_g.at[0], recv_g.at[0], to_gen).wait_recv()
        gen32 = unpack(gen_in[...].astype(f32))
        gen_out[...] = gen32[:, :C].astype(bf16)
        noise = sc[...].astype(f32)
        lev = level[...]
        noised = (1.0 - lev) * gen32 + lev * jnp.concatenate([noise, noise], axis=1)
        rows_in(noised.astype(bf16).astype(f32), lev)

        def deliver(value):
            out_pk[...] = pack(value).astype(bf16)
            copy = remote(out_pk, col_in.at[role], send_c.at[0], recv_c.at[role], to_gen)
            copy.start()
            return copy

        @pl.when(role == 3)
        def _():
            out = forward(True)
            logit = 0.5 * jnp.sum(out, axis=1, keepdims=True)
            down = -1.0 / (1.0 + jnp.exp(logit))
            through = back_acc[...]
            pulled = jnp.sum(z_aug[...].astype(f32) * through, axis=1, keepdims=True)
            latent = through[:, :128]
            latent = latent + pltpu.roll(latent, C, 1)
            inverse = rs[:, :128]
            back = inverse * latent - inverse * inverse * inverse * (1.0 / D) * pulled * y_ref[...]
            copy = deliver(adv_weight * (1.0 - level[...]) * down * back)
            cot[...] = jnp.broadcast_to(1.0 / (1.0 + jnp.exp(-logit)), (ROWS, 128))
            rows_turned()
            copy.wait_send()

        @pl.when(role != 3)
        def _():
            out = forward(False)
            copy = deliver(out)
            cot[...] = out - gen32

            @pl.when(role == 2)
            def _():
                slopes()
                rows_turned()

            copy.wait_send()

    @pl.when(role == 1)
    def _():
        grads[...] = jnp.zeros_like(grads)

    @pl.when(role != 1)
    def _():
        lane = lanes((ROWS, 128))
        full = cot[...]
        c_high = full.astype(bf16).astype(f32)
        cot2 = jnp.where(lane < C, c_high, full - c_high).astype(bf16)

        def body(c, carry):
            cs = columns(c)
            hcot = (dot_nt(cot2, r2[cs, :]) * slope[:, cs]).astype(bf16)
            x_ref[:, cs] = dot(z_t[...], hcot)
            return carry

        lax.fori_loop(0, CHUNKS, body, 0)
        x_ref[C : C + 1, :] = x_ref[C : C + 1, :] + x_ref[C + 1 : C + 2, :]
        stage_a_fill(t_a, False)
        h_a = stage_a(t_a, e_a, send_h, recv_h)
        start(h_a)
        arrive(h_a)
        summed = total(t_a[p], e_a)
        t_b[:, :HALF] = summed[:, :HALF].astype(bf16)
        v_high, v_low = split(summed[:, HALF : HALF + 128] + summed[:, HALF + 128 :])
        t_b[:, HALF : HALF + 128] = v_high
        t_b[:, HALF + 128 :] = v_low
        h_b = stage_b(t_b, e_b, send_h, recv_h)
        start(h_b)
        arrive(h_b)
        summed = total(summed, e_b)
        h_buf[pl.ds(own_top, 16), pl.ds(own_left, HALF)] = summed[:, :HALF].astype(bf16)
        h_c = stage_c(h_buf, send_h, recv_h)
        start(h_c)
        put_row(summed[:, HALF : HALF + 128] + summed[:, HALF + 128 :])
        left = lt[...] * (1.0 / math.sqrt(ROWS * SIDE * SIDE))
        l_high, l_low = split(left[:, :C])
        base = left[:, C : C + 1] * vrow[0:1, :]
        arrive(h_c)
        full_h = h_buf[...]
        grads[0] = base + dot(l_high, full_h) + dot(l_low, full_h)
        finish(h_a)
        finish(h_b)
        finish(h_c)


def shards(sn, sc, lv, emb, tim, gain, blk, rdo):
    vmem = pl.BlockSpec(memory_space=pltpu.VMEM)
    scratch = [
        ((80, F), f32), ((16, 128), f32), ((8, F), f32),
        ((SIDE, 16, HALF + 128), f32), ((SIDE, 16, HALF + 128), f32),
        ((16, HALF + 128), f32), ((SIDE, 16, HALF + 128), f32),
        ((C, F), f32), ((256, F), bf16),
        ((SIDE, 16, HALF + 256), bf16), ((SIDE, 16, HALF + 256), bf16),
        ((16, HALF + 256), bf16), ((SIDE, 16, HALF + 256), bf16), ((C, F), bf16),
        ((F, 128), bf16), ((256, 128), bf16), ((ROWS, 128), f32), ((ROWS, 128), f32),
        ((ROWS, 256), bf16), ((80, ROWS), bf16), ((ROWS, CHUNK), f32), ((ROWS, 128), f32),
        ((ROWS, F), f32), ((ROWS, F), f32), ((ROWS, 128), f32), ((ROWS, 256), f32),
        ((DEPTH, 128), f32), ((ROWS, 128), f32),
        ((ROWS // 2, 128), bf16), ((ROWS // 2, 128), bf16), ((ROWS // 2, 128), bf16),
        ((4, ROWS // 2, 128), bf16),
    ]
    dma = pltpu.SemaphoreType.DMA
    return pl.pallas_call(
        kernel,
        out_shape=(
            jax.ShapeDtypeStruct((1, DEPTH, F), f32),
            jax.ShapeDtypeStruct((ROWS, C), bf16),
        ),
        in_specs=[vmem] * 8,
        out_specs=(vmem, vmem),
        scratch_shapes=[pltpu.VMEM(shape, kind) for shape, kind in scratch]
        + [dma((3, SIDE)) for _ in range(4)]
        + [dma((4,)) for _ in range(4)],
        compiler_params=pltpu.CompilerParams(
            collective_id=0, has_side_effects=True, vmem_limit_bytes=48 * 2**20
        ),
    )(sn, sc, lv.reshape(ROWS // 128, 128), emb, tim, gain, blk, rdo)


def solution(mesh):
    in_specs = (
        P("fsdp", None),
        P("fsdp", None),
        P("fsdp"),
        P("role", None, None),
        P("role", None),
        P("role", None),
        P("role", "fsdp", None),
        P("role", None, None),
    )
    out_specs = (P("role", "fsdp", None), P("fsdp", None))
    return jax.shard_map(shards, mesh=mesh, in_specs=in_specs, out_specs=out_specs, check_vma=False)
```

time: 1400 us -> 74.6 us (0.05)
  waiting for transfers between devices: 1340 us -> 0 us
  Pallas kernels: 0 us -> 69.5 us
  matrix products: 27.8 us -> 0 us
    psum x2 -> x0, waiting for transfers between devices: 1340 us -> none  [the longest x1 673 us: shards(): lax.psum(jnp.dot(own, block_w.astype(jnp.float32), precision=HIGH), 'fsdp')]
    pallas_call x0 -> x1, Pallas kernels: none -> 69.5 us  [shards(): pl.pallas_call(kernel, out_shape=(jax.ShapeDtypeStruct((1, DEPTH, F), f32...]
    dot_general x13 -> x0, matrix products: 27.8 us -> none  [the longest x2 6.51 us: forward(): preact = jnp.dot(rows, lifted, precision=HIGH)]
  transfers between devices with their start and end apart: 2 -> 0, of which waited for: 2 -> 0; matrix products, arithmetic and copies ran while one was open for 0% -> 0% of each run, Pallas kernels for 0% -> 0%
where the time goes in v2:
time: 74.6 us; the launch traced here: 74.4 us
  Pallas kernels  69.5 us (93%)
  local copies, waits for them, and re-layouts  4.23 us (6%)
    pallas_call x1, Pallas kernels, shards(): pl.pallas_call(kernel, out_shape=(jax.ShapeDtypeStruct((1, DEPTH, F), f32...  69.5 us
    unnamed x16, local copies, waits for them, and re-layouts  3.52 us

profile of v2, /device:TPU:2, one launch (start us, length us, event | category | flops | bytes accessed | tf_op | source)
XLA Modules:
  0.0 74.4 jit_solution(4789952034964403779)
XLA Ops:
  0.6 0.0 copy-start.5
  0.6 1.0 %copy.10.sn = bf16[384,64]{1,0:T(8,128)(2,1)S(1)} copy(bf16[384,64]{0,1:T(8,128)(2,1)} %param.8) | data formatting | bytes 98304 | tf_op args[0]
  1.6 0.0 copy-start
  1.6 1.0 %copy.11.sc = bf16[384,64]{1,0:T(8,128)(2,1)S(1)} copy(bf16[384,64]{0,1:T(8,128)(2,1)} %param.9) | data formatting | bytes 98304 | tf_op args[1]
  2.6 0.0 copy-done.5
  2.6 0.0 copy-start.1
  2.6 0.0 copy-start.2
  2.6 0.0 copy-start.3
  2.6 0.0 copy-start.4
  2.6 0.2 copy.12.rdo
  2.9 0.0 copy-done
  2.9 0.6 copy-done.1
  3.5 0.0 copy-done.2
  3.5 0.0 copy-done.3
  3.5 0.0 copy-done.4
  3.5 69.5 %shard_map.95 = (f32[1,48,1536]{2,1,0:T(8,128)S(1)}, bf16[384,64]{1,0:T(8,128)(2,1)S(1)}) custom-call(bf16[384,64]{1,0:T(8,128)(2,1)S(1)} %copy.10.sn, bf16[384,64]{1,0:T(8,128)(2,1)S(1)} %copy.11.sc, f32[3,128]{1,0:T(4,128)S(1)} %bitcast.1, bf16[1,64,3072]{2,1,0:T(8,128)(2,1)S(1)} %copy-done, f32[1,3072]{1,0:T(1,128)S(1)} %copy-done.2, ...), custom_call_target="tpu_custom_call" | custom-call | tf_op jit(solution)/shard_map/pallas_call | solution.py:436
  73.0 0.7 copy.13
  73.7 0.7 copy.15
Async XLA Ops:
  0.6 2.0 %copy-start.5 = (bf16[1,1536,64]{1,2,0:T(8,128)(2,1)S(1)}, bf16[1,1536,64]{1,2,0:T(8,128)(2,1)}, u32[]{:S(2)}) copy-start(bf16[1,1536,64]{1,2,0:T(8,128)(2,1)} %param.15) | copy-start | bytes 589828
  1.6 1.3 %copy-start = (bf16[1,64,3072]{2,1,0:T(8,128)(2,1)S(1)}, bf16[1,64,3072]{2,1,0:T(8,128)(2,1)}, u32[]{:S(2)}) copy-start(bf16[1,64,3072]{2,1,0:T(8,128)(2,1)} %emb.1) | copy-start | bytes 1179652
  2.6 0.9 %copy-start.1 = (bf16[1,48,1536]{2,1,0:T(8,128)(2,1)S(1)}, bf16[1,48,1536]{2,1,0:T(8,128)(2,1)}, u32[]{:S(2)}) copy-start(bf16[1,48,1536]{2,1,0:T(8,128)(2,1)} %blk.1) | copy-start | bytes 442372
  2.6 0.9 %copy-start.2 = (f32[1,3072]{1,0:T(1,128)S(1)}, f32[1,3072]{1,0:T(1,128)}, u32[]{:S(2)}) copy-start(f32[1,3072]{1,0:T(1,128)} %tim.1) | copy-start | bytes 36868
  2.6 0.9 %copy-start.3 = (f32[1,3072]{1,0:T(1,128)S(1)}, f32[1,3072]{1,0:T(1,128)}, u32[]{:S(2)}) copy-start(f32[1,3072]{1,0:T(1,128)} %gain.1) | copy-start | bytes 36868
  2.6 0.9 %copy-start.4 = (f32[384]{0:T(512)S(1)}, f32[384]{0:T(512)}, u32[]{:S(2)}) copy-start(f32[384]{0:T(512)} %param.10) | copy-start | bytes 4612

commit v3 on v2

--- a/solution.py
+++ b/solution.py
@@ -20,6 +20,8 @@
 CHUNKS = F // CHUNK
 SIDE = 8
 HALF = F // 2
+YX_ORDER = (5, 3, 4, 7, 1, 6, 2)
+Z_ORDER = (4, 5, 3, 6, 2, 7, 1)
 ROOT = math.sqrt(2.0 / math.pi)
 CUBE = 0.044715 * ROOT
 
@@ -63,13 +65,19 @@
 
 
 def kernel(
-    sn, sc, lv, emb, tim, gain, blk, rdo,
-    grads, gen_out,
-    x_ref, vt, vrow, s_a, d_a, s_b, d_b, m_buf, m_aug,
+    *refs,
+):
+    hbm, (grads, gen_out), scratch, (fetch, *sems) = refs[:8], refs[8:10], refs[10:-10], refs[-10:]
+    step(hbm, fetch, grads, gen_out, *scratch, *sems)
+
+
+def step(
+    hbm, fetch, grads, gen_out,
+    sn, sc, lv, emb, tim, gain, blk, rdo, x_ref, vt, vrow, s_a, d_a, s_b, d_b, m_buf, m_aug,
     t_a, e_a, t_b, e_b, h_buf,
     r2, gram, level, z_f32, z_aug, z_t, rs, y_ref, hid, slope, acc, back_acc, lt, cot,
-    gen_pk, gen_in, out_pk, col_in,
-    send_m, recv_m, send_h, recv_h, send_g, recv_g, send_c, recv_c,
+    noise_in, gen_pk, gen_in, out_pk, col_in,
+    send_m, recv_m, send_h, recv_h, send_g, recv_g, send_c, recv_c, turn,
 ):
     role = lax.axis_index("role")
     place = lax.axis_index("fsdp")
@@ -85,11 +93,18 @@
         return (lax.rem(role + k, 4), place)
 
     barrier = pltpu.get_barrier_semaphore()
-    for k in range(1, SIDE):
-        pl.semaphore_signal(barrier, inc=1, device_id=yx_peer(k), device_id_type=MESH)
-        pl.semaphore_signal(barrier, inc=1, device_id=z_peer(k), device_id_type=MESH)
+    for k_yx, k_z in zip(YX_ORDER, Z_ORDER):
+        pl.semaphore_signal(barrier, inc=1, device_id=yx_peer(k_yx), device_id_type=MESH)
+        pl.semaphore_signal(barrier, inc=1, device_id=z_peer(k_z), device_id_type=MESH)
     for k in range(1, 4):
         pl.semaphore_signal(barrier, inc=1, device_id=role_peer(k), device_id_type=MESH)
+
+    fetches = [
+        pltpu.make_async_copy(src, dst, fetch.at[i])
+        for i, (src, dst) in enumerate(zip(hbm, (sn, sc, lv, emb, tim, gain, blk, rdo)))
+    ]
+    for i in (4, 5, 3, 6, 7, 0, 1, 2):
+        fetches[i].start()
 
     def remote(src, dst, send, recv, device):
         return pltpu.make_async_remote_copy(
@@ -101,6 +116,8 @@
     window = jnp.minimum(begin // 128, D // 128 - 2) * 128
     window = pl.multiple_of(window, 128)
     wide = pl.ds(window, 256)
+    for i in (4, 5, 3, 6):
+        fetches[i].wait()
     gain_w = gain[:, wide]
     lifted = jnp.concatenate(
         [
@@ -136,12 +153,12 @@
     def stage_a(send, dest, ss, rr):
         return [
             remote(send.at[lax.rem(p + k, SIDE)], dest.at[k], ss.at[0, k], rr.at[0, k], yx_peer(k))
-            for k in range(1, SIDE)
+            for k in YX_ORDER
         ]
 
     def stage_b(send, dest, ss, rr):
         return [
-            remote(send, dest.at[k], ss.at[1, k], rr.at[1, k], z_peer(k)) for k in range(1, SIDE)
+            remote(send, dest.at[k], ss.at[1, k], rr.at[1, k], z_peer(k)) for k in Z_ORDER
         ]
 
     own_top = pl.multiple_of(p // 2 * 16, 16)
@@ -149,7 +166,7 @@
 
     def stage_c(buf, ss, rr):
         own = buf.at[pl.ds(own_top, 16), pl.ds(own_left, HALF)]
-        return [remote(own, own, ss.at[2, k], rr.at[2, k], yx_peer(k)) for k in range(1, SIDE)]
+        return [remote(own, own, ss.at[2, k], rr.at[2, k], yx_peer(k)) for k in YX_ORDER]
 
     def start(copies):
         for copy in copies:
@@ -177,13 +194,21 @@
     stage_a_fill(s_a, True)
     pl.semaphore_wait(barrier, 2 * (SIDE - 1) + 3)
     m_a = stage_a(s_a, d_a, send_m, recv_m)
+
+    @pl.when((role == 1) | (role == 2))
+    def _():
+        pl.semaphore_wait(turn, 1)
+
     start(m_a)
+
+    for i in (0, 1, 2, 7):
+        fetches[i].wait()
 
     lt[...] = jnp.concatenate([lifted, jnp.zeros((48, 128), f32)], axis=0).T[:DEPTH]
     for i in range(ROWS // 128):
         level[i * 128 : i * 128 + 128, :] = jnp.broadcast_to(lv[i : i + 1, :], (128, 128)).T
     readout = rdo[0].astype(f32)
-    r2[...] = jnp.concatenate([readout, readout], axis=1).astype(bf16)
+    r2[...] = jnp.concatenate([readout, readout], axis=0).T.astype(bf16)
     time = tim[...]
     t_1 = time.astype(bf16).astype(f32)
     t_2 = (time - t_1).astype(bf16).astype(f32)
@@ -234,6 +259,13 @@
         z_t[...] = turned[:80].astype(bf16)
 
     arrive(m_a)
+
+    @pl.when((role == 0) | (role == 3))
+    def _():
+        pl.semaphore_signal(
+            turn, inc=1, device_id=(jnp.where(role == 0, 1, 2), place), device_id_type=MESH
+        )
+
     summed = total(s_a[p], d_a)
     s_b[...] = summed
     m_b = stage_b(s_b, d_b, send_m, recv_m)
@@ -243,7 +275,12 @@
     @pl.when(role == 0)
     def _():
         noise = sn[...].astype(f32)
-        rows_in(jnp.concatenate([noise, noise], axis=1), jnp.ones((ROWS, 128), f32))
+        rows_in(jnp.concatenate([noise, noise], axis=0).T, jnp.ones((ROWS, 128), f32))
+
+    @pl.when(role != 0)
+    def _():
+        noise = sc[...].astype(f32)
+        noise_in[...] = level[...] * jnp.concatenate([noise, noise], axis=0).T
 
     arrive(m_b)
     summed = total(summed, d_b)
@@ -281,13 +318,13 @@
             if critic:
                 rise = gelu_slope(square, half, value)
                 slope[:, cs] = rise * rs[...]
-                weight = dot_nt(jnp.ones((16, C), bf16), rdo[0, cs, :])[0:1, :]
+                weight = dot(jnp.ones((16, C), bf16), rdo[0, :, cs])[0:1, :]
                 back_acc[...] += dot_nt((rise * weight).astype(bf16), m_aug[:, cs])
             else:
                 hid[:, cs] = hidden
             return carry
 
-        lax.fori_loop(0, CHUNKS, body, 0)
+        lax.fori_loop(0, CHUNKS, body, 0, unroll=6)
         return acc[...].astype(bf16).astype(f32)
 
     def slopes():
@@ -296,7 +333,7 @@
             slope[:, cs] = gelu_slope(*gelu_parts(hid[:, cs])) * rs[...]
             return carry
 
-        lax.fori_loop(0, CHUNKS, body, 0)
+        lax.fori_loop(0, CHUNKS, body, 0, unroll=6)
 
     to_gen = (0, place)
 
@@ -308,7 +345,7 @@
             remote(gen_pk, gen_in, send_g.at[k], recv_g.at[0], (k, place)) for k in range(1, 4)
         ]
         start(copies)
-        gen_out[...] = out[:, :C].astype(bf16)
+        gen_out[...] = out.T[:C].astype(bf16)
         slopes()
         rows_turned()
         finish(copies)
@@ -328,10 +365,8 @@
     def _():
         remote(gen_pk, gen_in, send_g.at[0], recv_g.at[0], to_gen).wait_recv()
         gen32 = unpack(gen_in[...].astype(f32))
-        gen_out[...] = gen32[:, :C].astype(bf16)
-        noise = sc[...].astype(f32)
         lev = level[...]
-        noised = (1.0 - lev) * gen32 + lev * jnp.concatenate([noise, noise], axis=1)
+        noised = (1.0 - lev) * gen32 + noise_in[...]
         rows_in(noised.astype(bf16).astype(f32), lev)
 
         def deliver(value):
@@ -352,6 +387,7 @@
             inverse = rs[:, :128]
             back = inverse * latent - inverse * inverse * inverse * (1.0 / D) * pulled * y_ref[...]
             copy = deliver(adv_weight * (1.0 - level[...]) * down * back)
+            gen_out[...] = gen32.T[:C].astype(bf16)
             cot[...] = jnp.broadcast_to(1.0 / (1.0 + jnp.exp(-logit)), (ROWS, 128))
             rows_turned()
             copy.wait_send()
@@ -360,6 +396,7 @@
         def _():
             out = forward(False)
             copy = deliver(out)
+            gen_out[...] = gen32.T[:C].astype(bf16)
             cot[...] = out - gen32
 
             @pl.when(role == 2)
@@ -386,7 +423,7 @@
             x_ref[:, cs] = dot(z_t[...], hcot)
             return carry
 
-        lax.fori_loop(0, CHUNKS, body, 0)
+        lax.fori_loop(0, CHUNKS, body, 0, unroll=6)
         x_ref[C : C + 1, :] = x_ref[C : C + 1, :] + x_ref[C + 1 : C + 2, :]
         stage_a_fill(t_a, False)
         h_a = stage_a(t_a, e_a, send_h, recv_h)
@@ -419,6 +456,8 @@
 def shards(sn, sc, lv, emb, tim, gain, blk, rdo):
     vmem = pl.BlockSpec(memory_space=pltpu.VMEM)
     scratch = [
+        ((C, ROWS), bf16), ((C, ROWS), bf16), ((ROWS // 128, 128), f32), ((1, C, D), bf16),
+        ((1, D), f32), ((1, D), f32), ((1, DEPTH, F), bf16), ((1, C, F), bf16),
         ((80, F), f32), ((16, 128), f32), ((8, F), f32),
         ((SIDE, 16, HALF + 128), f32), ((SIDE, 16, HALF + 128), f32),
         ((16, HALF + 128), f32), ((SIDE, 16, HALF + 128), f32),
@@ -429,25 +468,29 @@
         ((ROWS, 256), bf16), ((80, ROWS), bf16), ((ROWS, CHUNK), f32), ((ROWS, 128), f32),
         ((ROWS, F), f32), ((ROWS, F), f32), ((ROWS, 128), f32), ((ROWS, 256), f32),
         ((DEPTH, 128), f32), ((ROWS, 128), f32),
+        ((ROWS, 128), f32),
         ((ROWS // 2, 128), bf16), ((ROWS // 2, 128), bf16), ((ROWS // 2, 128), bf16),
         ((4, ROWS // 2, 128), bf16),
     ]
     dma = pltpu.SemaphoreType.DMA
-    return pl.pallas_call(
+    grads, generated = pl.pallas_call(
         kernel,
         out_shape=(
             jax.ShapeDtypeStruct((1, DEPTH, F), f32),
-            jax.ShapeDtypeStruct((ROWS, C), bf16),
+            jax.ShapeDtypeStruct((C, ROWS), bf16),
         ),
-        in_specs=[vmem] * 8,
+        in_specs=[pl.BlockSpec(memory_space=pltpu.HBM)] * 8,
         out_specs=(vmem, vmem),
         scratch_shapes=[pltpu.VMEM(shape, kind) for shape, kind in scratch]
+        + [dma((8,))]
         + [dma((3, SIDE)) for _ in range(4)]
-        + [dma((4,)) for _ in range(4)],
+        + [dma((4,)) for _ in range(4)]
+        + [pltpu.SemaphoreType.REGULAR],
         compiler_params=pltpu.CompilerParams(
-            collective_id=0, has_side_effects=True, vmem_limit_bytes=48 * 2**20
+            collective_id=0, has_side_effects=True, vmem_limit_bytes=64 * 2**20
         ),
-    )(sn, sc, lv.reshape(ROWS // 128, 128), emb, tim, gain, blk, rdo)
+    )(sn.T, sc.T, lv.reshape(ROWS // 128, 128), emb, tim, gain, blk, rdo.transpose(0, 2, 1))
+    return grads, generated.T
 
 
 def solution(mesh):

time: 74.6 us -> 66.6 us (0.89)
  Pallas kernels: 69.5 us -> 63.1 us
  local copies, waits for them, and re-layouts: 4.23 us -> 2.33 us
    pallas_call x1, Pallas kernels: 69.5 us -> 63.1 us  [shards(): pl.pallas_call(kernel, out_shape=(jax.ShapeDtypeStruct((1, DEPTH, F), f32...]
    unnamed x16 -> x4, local copies, waits for them, and re-layouts: 3.52 us -> 2.33 us
where the time goes in v3:
time: 66.6 us; the launch traced here: 66 us
  Pallas kernels  63.1 us (95%)
  local copies, waits for them, and re-layouts  2.33 us (3%)
    pallas_call x1, Pallas kernels, shards(): pl.pallas_call(kernel, out_shape=(jax.ShapeDtypeStruct((1, DEPTH, F), f32...  63.1 us
    unnamed x4, local copies, waits for them, and re-layouts  2.33 us

profile of v3, /device:TPU:2, one launch (start us, length us, event | category | flops | bytes accessed | tf_op | source)
XLA Modules:
  0.0 66.0 jit_solution(17968088017461995801)
XLA Ops:
  0.6 63.1 %shard_map.95 = (f32[1,48,1536]{2,1,0:T(8,128)}, bf16[64,384]{1,0:T(8,128)(2,1)}) custom-call(bf16[64,384]{1,0:T(8,128)(2,1)} %bitcast.7, bf16[64,384]{1,0:T(8,128)(2,1)} %bitcast.8, f32[3,128]{1,0:T(4,128)} %bitcast.9, bf16[1,64,3072]{2,1,0:T(8,128)(2,1)} %refs_3_.1, f32[1,3072]{1,0:T(1,128)} %refs_4_.1, f32[1,3072]{1,0:T(1,128)} %refs_5_.1, ...), custom_call_target="tpu_custom_call" | custom-call | tf_op jit(solution)/shard_map/pallas_call | solution.py:476
  63.7 0.0 copy-start
  63.7 1.7 %copy.12 = f32[1,48,1536]{2,1,0:T(8,128)} copy(f32[1,48,1536]{2,1,0:T(8,128)} %get-tuple-element.8) | data formatting | bytes 589824
  65.4 0.0 copy-done
  65.4 0.6 copy.13
Async XLA Ops:
  63.7 1.7 %copy-start = (bf16[64,384]{1,0:T(8,128)(2,1)S(1)}, bf16[64,384]{1,0:T(8,128)(2,1)}, u32[]{:S(2)}) copy-start(bf16[64,384]{1,0:T(8,128)(2,1)} %get-tuple-element.5) | copy-start | bytes 147460

commit v4 on v3

--- a/solution.py
+++ b/solution.py
@@ -191,7 +191,7 @@
         for i in range(F // 128):
             vrow[0:1, i * 128 : i * 128 + 128] = vt[i : i + 1, :]
 
-    stage_a_fill(s_a, True)
+    stage_a_fill(s_a, False)
     pl.semaphore_wait(barrier, 2 * (SIDE - 1) + 3)
     m_a = stage_a(s_a, d_a, send_m, recv_m)
 
@@ -267,7 +267,10 @@
         )
 
     summed = total(s_a[p], d_a)
-    s_b[...] = summed
+    s_b[:, :HALF] = summed[:, :HALF].astype(bf16)
+    v_high, v_low = split(summed[:, HALF : HALF + 128] + summed[:, HALF + 128 :])
+    s_b[:, HALF : HALF + 128] = v_high
+    s_b[:, HALF + 128 :] = v_low
     m_b = stage_b(s_b, d_b, send_m, recv_m)
     start(m_b)
     m_aug[128 + 16 :, :] = jnp.zeros((128 - 16, F), bf16)
@@ -284,10 +287,10 @@
 
     arrive(m_b)
     summed = total(summed, d_b)
-    m_buf[pl.ds(own_top, 16), pl.ds(own_left, HALF)] = summed[:, :HALF]
+    m_buf[pl.ds(own_top, 16), pl.ds(own_left, HALF)] = summed[:, :HALF].astype(bf16)
     m_c = stage_c(m_buf, send_m, recv_m)
     start(m_c)
-    put_row(summed[:, HALF:])
+    put_row(summed[:, HALF : HALF + 128] + summed[:, HALF + 128 :])
     v_full = vrow[0:1, :]
     v_high = v_full.astype(bf16).astype(f32)
     rows = lax.broadcasted_iota(jnp.int32, (16, F), 0)
@@ -295,9 +298,8 @@
         (rows == 0) | (rows == 2), v_high, jnp.where(rows == 1, v_full - v_high, 0.0)
     ).astype(bf16)
     arrive(m_c)
-    high, low = split(m_buf[...])
-    m_aug[0:64, :] = high
-    m_aug[64:128, :] = low
+    m_aug[0:64, :] = m_buf[...]
+    m_aug[64:128, :] = jnp.zeros((64, F), bf16)
     finish(m_a)
     finish(m_b)
     finish(m_c)
@@ -459,9 +461,9 @@
         ((C, ROWS), bf16), ((C, ROWS), bf16), ((ROWS // 128, 128), f32), ((1, C, D), bf16),
         ((1, D), f32), ((1, D), f32), ((1, DEPTH, F), bf16), ((1, C, F), bf16),
         ((80, F), f32), ((16, 128), f32), ((8, F), f32),
-        ((SIDE, 16, HALF + 128), f32), ((SIDE, 16, HALF + 128), f32),
-        ((16, HALF + 128), f32), ((SIDE, 16, HALF + 128), f32),
-        ((C, F), f32), ((256, F), bf16),
+        ((SIDE, 16, HALF + 256), bf16), ((SIDE, 16, HALF + 256), bf16),
+        ((16, HALF + 256), bf16), ((SIDE, 16, HALF + 256), bf16),
+        ((C, F), bf16), ((256, F), bf16),
         ((SIDE, 16, HALF + 256), bf16), ((SIDE, 16, HALF + 256), bf16),
         ((16, HALF + 256), bf16), ((SIDE, 16, HALF + 256), bf16), ((C, F), bf16),
         ((F, 128), bf16), ((256, 128), bf16), ((ROWS, 128), f32), ((ROWS, 128), f32),
@@ -487,9 +489,17 @@
         + [dma((4,)) for _ in range(4)]
         + [pltpu.SemaphoreType.REGULAR],
         compiler_params=pltpu.CompilerParams(
-            collective_id=0, has_side_effects=True, vmem_limit_bytes=64 * 2**20
+            collective_id=0, has_side_effects=True, vmem_limit_bytes=32 * 2**20
         ),
-    )(sn.T, sc.T, lv.reshape(ROWS // 128, 128), emb, tim, gain, blk, rdo.transpose(0, 2, 1))
+    )(
+        *(
+            pltpu.with_memory_space_constraint(array, pltpu.HBM)
+            for array in (
+                sn.T, sc.T, lv.reshape(ROWS // 128, 128), emb, tim, gain, blk,
+                rdo.transpose(0, 2, 1),
+            )
+        )
+    )
     return grads, generated.T
 
 

time: 66.6 us -> 59.6 us (0.89)
  Pallas kernels: 63.1 us -> 57.5 us
  local copies, waits for them, and re-layouts: 2.33 us -> 1.34 us
    pallas_call x1, Pallas kernels: 63.1 us -> 57.5 us  [shards(): pl.pallas_call(kernel, out_shape=(jax.ShapeDtypeStruct((1, DEPTH, F), f32...]
    unnamed x4 -> x2, local copies, waits for them, and re-layouts: 2.33 us -> 1.34 us
where the time goes in v4:
time: 59.6 us; the launch traced here: 59.5 us
  Pallas kernels  57.5 us (96%)
  local copies, waits for them, and re-layouts  1.34 us (2%)
  between operations  0.64 us (1%)
    pallas_call x1, Pallas kernels, shards(): pl.pallas_call(kernel, out_shape=(jax.ShapeDtypeStruct((1, DEPTH, F), f32...  57.5 us
    unnamed x2, local copies, waits for them, and re-layouts  1.34 us

profile of v4, /device:TPU:2, one launch (start us, length us, event | category | flops | bytes accessed | tf_op | source)
XLA Modules:
  0.0 59.5 jit_solution(11726546490645928464)
XLA Ops:
  0.6 57.5 %shard_map.95 = (f32[1,48,1536]{2,1,0:T(8,128)S(1)}, bf16[64,384]{1,0:T(8,128)(2,1)S(1)}) custom-call(bf16[64,384]{1,0:T(8,128)(2,1)} %bitcast.7, bf16[64,384]{1,0:T(8,128)(2,1)} %bitcast.8, f32[3,128]{1,0:T(4,128)} %bitcast.9, bf16[1,64,3072]{2,1,0:T(8,128)(2,1)} %refs_3_.1, f32[1,3072]{1,0:T(1,128)} %refs_4_.1, f32[1,3072]{1,0:T(1,128)} %refs_5_.1, ...), custom_call_target="tpu_custom_call" | custom-call | tf_op jit(solution)/shard_map/pallas_call | solution.py:478
  58.1 0.7 %copy.12 = f32[1,48,1536]{2,1,0:T(8,128)} copy(f32[1,48,1536]{2,1,0:T(8,128)S(1)} %get-tuple-element.8) | data formatting | bytes 589824
  58.9 0.6 %copy.13 = bf16[384,64]{0,1:T(8,128)(2,1)} copy(bf16[384,64]{0,1:T(8,128)(2,1)S(1)} %bitcast.5) | data formatting | bytes 98304

commit v5 on v4

v5 whole, which is shorter than its diff:
```python
import functools
import math

import jax
import jax.numpy as jnp
from jax import lax
from jax.experimental import pallas as pl
from jax.experimental.pallas import tpu as pltpu
from jax.sharding import PartitionSpec as P

MESH = pl.DeviceIdType.MESH
f32, bf16 = jnp.float32, jnp.bfloat16
adv_weight = 3.0
ROWS = 384
C = 64
D = 3072
F = 1536
DEPTH = 48
CHUNK = 256
CHUNKS = F // CHUNK
SIDE = 8
HALF = F // 2
YX_ORDER = (5, 3, 4, 7, 1, 6, 2)
Z_ORDER = (4, 5, 3, 6, 2, 7, 1)
ROOT = math.sqrt(2.0 / math.pi)
CUBE = 0.044715 * ROOT


def dot(a, b):
    return jnp.dot(a, b, preferred_element_type=f32)


def dot_nt(a, b):
    return lax.dot_general(a, b, (((1,), (1,)), ((), ())), preferred_element_type=f32)


def split(value):
    high = value.astype(bf16)
    return high, (value - high.astype(f32)).astype(bf16)


def lanes(shape):
    return lax.broadcasted_iota(jnp.int32, shape, len(shape) - 1)


def pack(value):
    top, bottom = value[: ROWS // 2], value[ROWS // 2 :]
    return jnp.where(lanes(top.shape) < C, top, bottom)


def unpack(value):
    turned = pltpu.roll(value, C, 1)
    left = lanes(value.shape) < C
    return jnp.concatenate([jnp.where(left, value, turned), jnp.where(left, turned, value)], axis=0)


def gelu_parts(hidden):
    square = hidden * hidden
    half = 0.5 + 0.5 * jnp.tanh(hidden * (ROOT + CUBE * square))
    return square, half, hidden * half


def gelu_slope(square, half, value):
    return half + value * (1.0 - half) * (2.0 * ROOT + 6.0 * CUBE * square)


def kernel(
    *refs,
):
    hbm, (grads, gen_out), scratch, (fetch, *sems) = refs[:8], refs[8:10], refs[10:-12], refs[-12:]
    step(hbm, fetch, grads, gen_out, *scratch, *sems)


def step(
    hbm, fetch, grads, gen_out,
    sn, sc, lv, emb, tim, gain, blk, rdo, x_ref, vt, vrow, s_a, d_a, s_b, d_b, m_all, rsum, gen_f, rd_in, rs_row, rs_in,
    t_a, e_a, t_b, e_b, h_buf,
    r2_all, gram, level, z_f32, z_all, z_t, rs_all, y_ref, hid, slope, lt, cot,
    noise_in, gen_pk, gen_in, out_pk, col_in,
    send_m, recv_m, send_h, recv_h, send_g, recv_g, send_c, recv_c, send_x, recv_x, turn,
):
    role = lax.axis_index("role")
    place = lax.axis_index("fsdp")
    p, z = place // SIDE, place % SIDE
    slot = jnp.where(role == 0, 0, 1)

    def yx_peer(k):
        return (role, lax.rem(p + k, SIDE) * SIDE + z)

    def z_peer(k):
        return (role, p * SIDE + lax.rem(z + k, SIDE))

    def role_peer(k):
        return (lax.rem(role + k, 4), place)

    barrier = pltpu.get_barrier_semaphore()
    for k_yx, k_z in zip(YX_ORDER, Z_ORDER):
        pl.semaphore_signal(barrier, inc=1, device_id=yx_peer(k_yx), device_id_type=MESH)
        pl.semaphore_signal(barrier, inc=1, device_id=z_peer(k_z), device_id_type=MESH)
    for k in range(1, 4):
        pl.semaphore_signal(barrier, inc=1, device_id=role_peer(k), device_id_type=MESH)

    fetches = [
        pltpu.make_async_copy(src, dst, fetch.at[i])
        for i, (src, dst) in enumerate(zip(hbm, (sn, sc, lv, emb, tim, gain, blk, rdo)))
    ]
    for i in (4, 5, 3, 6, 7, 0, 1, 2):
        fetches[i].start()

    def remote(src, dst, send, recv, device):
        return pltpu.make_async_remote_copy(
            src_ref=src, dst_ref=dst, send_sem=send, recv_sem=recv, device_id=device,
            device_id_type=MESH,
        )

    begin = place * DEPTH
    window = jnp.minimum(begin // 128, D // 128 - 2) * 128
    window = pl.multiple_of(window, 128)
    wide = pl.ds(window, 256)
    for i in (4, 5, 3, 6):
        fetches[i].wait()
    gain_w = gain[:, wide]
    lifted = jnp.concatenate(
        [
            emb[0, :, wide].astype(f32) * gain_w,
            jnp.where(
                lax.broadcasted_iota(jnp.int32, (16, 256), 0) == 0, tim[:, wide] * gain_w, 0.0
            ),
        ],
        axis=0,
    )
    lifted = pltpu.roll(lifted, lax.rem(256 + window - begin, 256), 1)[:, :128]
    high, low = split(lifted[:, :DEPTH])
    block = blk[0]
    x_ref[...] = dot(high, block) + dot(low, block)

    def stage_a_fill(send, low_too):
        vt[...] = jnp.zeros_like(vt)
        for i in range(F // 128):
            vt[i : i + 1, :] = x_ref[C : C + 1, i * 128 : i * 128 + 128]
        tile = vt[...]
        for piece in range(SIDE):
            top, left = piece // 2 * 16, piece % 2 * HALF
            send[piece, :, :HALF] = x_ref[top : top + 16, left : left + HALF].astype(bf16)
            v_high, v_low = split(tile)
            send[piece, :, HALF : HALF + 128] = v_high
            if low_too:
                send[piece, :, HALF + 128 :] = v_low

    def stage_a(send, dest, ss, rr):
        return [
            remote(send.at[lax.rem(p + k, SIDE)], dest.at[k], ss.at[0, k], rr.at[0, k], yx_peer(k))
            for k in YX_ORDER
        ]

    def stage_b(send, dest, ss, rr):
        return [
            remote(send, dest.at[k], ss.at[1, k], rr.at[1, k], z_peer(k)) for k in Z_ORDER
        ]

    own_top = pl.multiple_of(p // 2 * 16, 16)
    own_left = pl.multiple_of(lax.rem(p, 2) * HALF, 128)

    other_left = pl.multiple_of(HALF - own_left, 128)
    own_block = (pl.ds(own_top, 16), pl.ds(own_left, HALF))

    def stage_c(buf, ss, rr):
        own = buf.at[own_block]
        return [remote(own, own, ss.at[2, k], rr.at[2, k], yx_peer(k)) for k in YX_ORDER]

    def start(copies):
        for copy in copies:
            copy.start()

    def arrive(copies):
        for copy in copies:
            copy.wait_recv()

    def finish(copies):
        for copy in copies:
            copy.wait_send()

    def total(first, dest):
        value = first.astype(f32)
        for k in range(1, SIDE):
            value = value + dest[k].astype(f32)
        return value

    def put_row(tile):
        vt[...] = tile
        for i in range(F // 128):
            vrow[0:1, i * 128 : i * 128 + 128] = vt[i : i + 1, :]

    stage_a_fill(s_a, True)
    pl.semaphore_wait(barrier, 2 * (SIDE - 1) + 3)
    m_a = stage_a(s_a, d_a, send_m, recv_m)

    @pl.when(role == 1)
    def _():
        pl.semaphore_wait(turn, 1)

    start(m_a)

    for i in (0, 1, 2, 7):
        fetches[i].wait()

    lt[...] = jnp.concatenate([lifted, jnp.zeros((48, 128), f32)], axis=0).T[:DEPTH]
    for i in range(ROWS // 128):
        level[i * 128 : i * 128 + 128, :] = jnp.broadcast_to(lv[i : i + 1, :], (128, 128)).T
    readout = rdo[0].astype(f32)
    rsum[...] = dot(jnp.ones((16, C), bf16), rdo[0])[:8]
    r2_all[slot] = jnp.concatenate([readout, readout], axis=0).T.astype(bf16)
    time = tim[...]
    t_1 = time.astype(bf16).astype(f32)
    t_2 = (time - t_1).astype(bf16).astype(f32)
    t_3 = time - t_1 - t_2
    rows = lax.broadcasted_iota(jnp.int32, (16, D), 0)
    parts = jnp.where(rows == 0, t_1, jnp.where(rows == 1, t_2, jnp.where(rows == 2, t_3, 0.0)))
    square_e = dot_nt(emb[0], emb[0])
    cross = jnp.sum(dot_nt(parts.astype(bf16), emb[0]), axis=0, keepdims=True)
    square_e = jnp.concatenate([square_e, square_e], axis=1)
    cross = jnp.concatenate([cross, cross], axis=1)
    square_t = jnp.sum(time * time, axis=1, keepdims=True)
    g_1, rest = split(square_e)
    rest = square_e - g_1.astype(f32)
    g_2, g_3 = split(rest)
    for i, part in enumerate((g_1, g_2, g_3)):
        gram[i, :C] = part
        gram[i, C:] = jnp.zeros((C, 128), bf16)
    m_all[0, 80:, :] = jnp.zeros((48, F), bf16)
    m_all[1, 80:, :] = jnp.zeros((48, F), bf16)

    def rows_with(latent, lev):
        lane = lanes((ROWS, 128))
        lev_high = lev.astype(bf16).astype(f32)
        return jnp.where(
            lane < C,
            latent,
            jnp.where(lane < C + 2, lev_high, jnp.where(lane == C + 2, lev - lev_high, 0.0)),
        ).astype(bf16)

    def rows_in(to, latent, lev):
        z_f32[...] = latent
        z16 = rows_with(latent, lev)
        z_all[to] = z16
        y = dot(z16, gram[0]) + dot(z16, gram[1]) + dot(z16, gram[2]) + lev * cross
        y_ref[...] = y
        mean = (
            0.5 * jnp.sum(latent * (y + lev * cross), axis=1, keepdims=True)
            + lev[:, :1] * lev[:, :1] * square_t
        ) * (1.0 / D)
        rs_all[to] = jnp.broadcast_to(lax.rsqrt(jnp.maximum(mean, 0.0) + 1e-06), (ROWS, CHUNK))

    def rows_turned():
        lane = lanes((ROWS, 128))
        lev = jnp.where(role == 0, 1.0, level[...])
        lev_high = lev.astype(bf16).astype(f32)
        turned = jnp.where(
            lane < C,
            z_f32[...],
            jnp.where(lane == C, lev_high, jnp.where(lane == C + 1, lev - lev_high, 0.0)),
        ).T
        z_t[...] = turned[:80].astype(bf16)

    critic_here = (3, place)
    x_readout = remote(rdo.at[0], rd_in, send_x.at[8], recv_x.at[8], critic_here)
    x_scales = remote(rs_row, rs_in, send_x.at[9], recv_x.at[9], critic_here)
    level_rows = m_all.at[0, pl.ds(C, 16), :]
    x_level = remote(level_rows, level_rows, send_x.at[10], recv_x.at[10], critic_here)
    matrix_block = m_all.at[(0, *own_block)]
    x_matrix = {
        k: remote(
            matrix_block, matrix_block, send_x.at[k], recv_x.at[k],
            (3, lax.rem(p + k, SIDE) * SIDE + z),
        )
        for k in (*YX_ORDER, 0)
    }

    arrive(m_a)

    @pl.when(role == 0)
    def _():
        pl.semaphore_signal(
            turn, inc=1, device_id=(jnp.where(role == 0, 1, 2), place), device_id_type=MESH
        )

    summed = total(s_a[p], d_a)
    s_b[:, :HALF] = summed[:, :HALF].astype(bf16)
    v_high, v_low = split(summed[:, HALF : HALF + 128] + summed[:, HALF + 128 :])
    s_b[:, HALF : HALF + 128] = v_high
    s_b[:, HALF + 128 :] = v_low
    m_b = stage_b(s_b, d_b, send_m, recv_m)
    start(m_b)

    @pl.when((role == 0) | (role == 3))
    def _():
        noise = sn[...].astype(f32)
        noise = jnp.concatenate([noise, noise], axis=0).T

        @pl.when(role == 0)
        def _():
            x_readout.start()
            rows_in(0, noise, jnp.ones((ROWS, 128), f32))
            rs_row[...] = rs_all[0, :, :128].T[:8]
            x_scales.start()

        @pl.when(role == 3)
        def _():
            z_all[0] = rows_with(noise, jnp.ones((ROWS, 128), f32))

    @pl.when(role != 0)
    def _():
        noise = sc[...].astype(f32)
        noise_in[...] = level[...] * jnp.concatenate([noise, noise], axis=0).T

    arrive(m_b)
    summed = total(summed, d_b)
    m_all[(slot, *own_block)] = summed[:, :HALF].astype(bf16)
    m_c = dict(zip(YX_ORDER, stage_c(m_all.at[slot], send_m, recv_m)))
    for k in YX_ORDER:
        m_c[k].start()

        @pl.when(role == 0)
        def _():
            x_matrix[k].start()

    put_row(summed[:, HALF : HALF + 128] + summed[:, HALF + 128 :])
    v_full = vrow[0:1, :]
    v_high = v_full.astype(bf16).astype(f32)
    rows = lax.broadcasted_iota(jnp.int32, (16, F), 0)
    m_all[slot, C : C + 16, :] = jnp.where(
        (rows == 0) | (rows == 2), v_high, jnp.where(rows == 1, v_full - v_high, 0.0)
    ).astype(bf16)

    @pl.when(role == 0)
    def _():
        x_level.start()
        x_matrix[0].start()

    near, far = (2, 4, 6), (1, 3, 5, 7)

    @pl.when(role != 0)
    def _():
        arrive(m_c.values())

    @pl.when(role == 3)
    def _():
        x_readout.wait_recv()
        first = rd_in[...].astype(f32)
        r2_all[0] = jnp.concatenate([first, first], axis=0).T.astype(bf16)
        x_scales.wait_recv()
        for i in range(ROWS // 128):
            here = slice(i * 128, i * 128 + 128)
            scales = jnp.broadcast_to(rs_in[0:1, here], (128, 128)).T
            rs_all[0, here, :128] = scales
            rs_all[0, here, 128:] = scales
        x_level.wait_recv()

    def columns(c):
        left = own_left if c < CHUNKS // 2 else other_left
        return pl.ds(pl.multiple_of(left + c % (CHUNKS // 2) * CHUNK, CHUNK), CHUNK)

    def forward(net, critic, before=None):
        out = jnp.zeros((ROWS, 128), f32)
        through = jnp.zeros((ROWS, 128), f32)
        for c in range(CHUNKS):
            if before and c % (CHUNKS // 2) == 0:
                before(c)
            cs = columns(c)
            hidden = dot(z_all[net], m_all[net, :, cs]) * rs_all[net]
            square, half, value = gelu_parts(hidden)
            out += dot(value.astype(bf16), r2_all[net, cs, :])
            if critic:
                rise = gelu_slope(square, half, value)
                slope[:, cs] = rise * rs_all[net]
                through += dot_nt((rise * rsum[0:1, cs]).astype(bf16), m_all[net, :, cs])
            else:
                hid[:, cs] = hidden
        return out.astype(bf16).astype(f32), through

    def slopes():
        for c in range(CHUNKS):
            cs = pl.ds(c * CHUNK, CHUNK)
            slope[:, cs] = gelu_slope(*gelu_parts(hid[:, cs])) * rs_all[slot]

    hand_on = remote(
        gen_pk, gen_in, send_g.at[0], recv_g.at[0], (jnp.where(role == 0, 1, 2), place)
    )

    def to_gen(source, device):
        return remote(
            out_pk, col_in.at[source], send_c.at[0], recv_c.at[source], (device, place)
        )

    @pl.when((role == 0) | (role == 3))
    def _():
        def matrix_in(c):
            @pl.when(role == 0)
            def _():
                arrive([m_c[k] for k in (near if c == 0 else far)])

            @pl.when(role == 3)
            def _():
                arrive([x_matrix[k] for k in ((0, *near) if c == 0 else far)])

        out, unused = forward(0, False, matrix_in)
        gen_f[...] = out
        gen_pk[...] = pack(out).astype(bf16)
        hand_on.start()

    @pl.when(role == 0)
    def _():
        gen_out[...] = gen_f[...].T[:C].astype(bf16)
        slopes()
        rows_turned()
        finish(x_matrix.values())
        finish((x_readout, x_scales, x_level, hand_on))

    @pl.when(role != 0)
    def _():
        @pl.when(role != 3)
        def _():
            hand_on.wait_recv()
            gen_f[...] = unpack(gen_in[...].astype(f32))

        lev = level[...]
        noised = (1.0 - lev) * gen_f[...] + noise_in[...]
        rows_in(1, noised.astype(bf16).astype(f32), lev)

        @pl.when(role == 3)
        def _():
            out, through = forward(1, True)
            logit = 0.5 * jnp.sum(out, axis=1, keepdims=True)
            down = -1.0 / (1.0 + jnp.exp(logit))
            pulled = jnp.sum(z_all[1].astype(f32) * through, axis=1, keepdims=True)
            latent = jnp.where(lanes((ROWS, 128)) < C, through, pltpu.roll(through, C, 1))
            inverse = rs_all[1, :, :128]
            back = inverse * (latent - inverse * inverse * (1.0 / D) * pulled * y_ref[...])
            out_pk[...] = pack(adv_weight * (1.0 - lev) * down * back).astype(bf16)
            to_gen(3, 0).start()
            cot[...] = jnp.broadcast_to(1.0 / (1.0 + jnp.exp(-logit)), (ROWS, 128))
            hand_on.wait_send()

        @pl.when(role != 3)
        def _():
            out, unused = forward(1, False)
            out_pk[...] = pack(out).astype(bf16)
            to_gen(role, 0).start()
            cot[...] = out - gen_f[...]

        @pl.when(role == 2)
        def _():
            slopes()

        rows_turned()
        gen_out[...] = gen_f[...].T[:C].astype(bf16)
        to_gen(role, 0).wait_send()

    finish(m_a)
    finish(m_b)
    finish(m_c.values())

    @pl.when(role == 1)
    def _():
        grads[...] = jnp.zeros_like(grads)

    @pl.when(role == 0)
    def _():
        for source in (1, 2, 3):
            to_gen(source, source).wait_recv()
        real, fake, adversarial = [unpack(col_in[k].astype(f32)) for k in (1, 2, 3)]
        gen32 = gen_f[...]
        spread = jnp.sum(jnp.abs(gen32 - real), axis=1, keepdims=True) * (0.5 / C) + 1e-05
        dmd = ((fake - real) / spread).astype(bf16).astype(f32)
        cot[...] = dmd + adversarial

    @pl.when(role != 1)
    def _():
        lane = lanes((ROWS, 128))
        full = cot[...]
        c_high = full.astype(bf16).astype(f32)
        cot2 = jnp.where(lane < C, c_high, full - c_high).astype(bf16)
        for c in range(CHUNKS):
            cs = pl.ds(c * CHUNK, CHUNK)
            hcot = (dot_nt(cot2, r2_all[slot, cs, :]) * slope[:, cs]).astype(bf16)
            x_ref[:, cs] = dot(z_t[...], hcot)
        x_ref[C : C + 1, :] = x_ref[C : C + 1, :] + x_ref[C + 1 : C + 2, :]
        stage_a_fill(t_a, False)
        h_a = stage_a(t_a, e_a, send_h, recv_h)
        start(h_a)
        arrive(h_a)
        summed = total(t_a[p], e_a)
        t_b[...] = summed.astype(bf16)
        h_b = stage_b(t_b, e_b, send_h, recv_h)
        start(h_b)
        arrive(h_b)
        summed = total(summed, e_b)
        h_buf[pl.ds(own_top, 16), pl.ds(own_left, HALF)] = summed[:, :HALF].astype(bf16)
        h_c = stage_c(h_buf, send_h, recv_h)
        start(h_c)
        put_row(summed[:, HALF:])
        left = lt[...] * (1.0 / math.sqrt(ROWS * SIDE * SIDE))
        l_high, l_low = split(left[:, :C])
        base = left[:, C : C + 1] * vrow[0:1, :]
        arrive(h_c)
        full_h = h_buf[...]
        grads[0] = base + dot(l_high, full_h) + dot(l_low, full_h)
        finish(h_a)
        finish(h_b)
        finish(h_c)


def shards(sn, sc, lv, emb, tim, gain, blk, rdo):
    vmem = pl.BlockSpec(memory_space=pltpu.VMEM)
    scratch = [
        ((C, ROWS), bf16), ((C, ROWS), bf16), ((ROWS // 128, 128), f32), ((1, C, D), bf16),
        ((1, D), f32), ((1, D), f32), ((1, DEPTH, F), bf16), ((1, C, F), bf16),
        ((80, F), f32), ((16, 128), f32), ((8, F), f32),
        ((SIDE, 16, HALF + 256), bf16), ((SIDE, 16, HALF + 256), bf16),
        ((16, HALF + 256), bf16), ((SIDE, 16, HALF + 256), bf16),
        ((2, 128, F), bf16), ((8, F), f32), ((ROWS, 128), f32),
        ((C, F), bf16), ((8, ROWS), f32), ((8, ROWS), f32),
        ((SIDE, 16, HALF + 128), bf16), ((SIDE, 16, HALF + 128), bf16),
        ((16, HALF + 128), bf16), ((SIDE, 16, HALF + 128), bf16), ((C, F), bf16),
        ((2, F, 128), bf16), ((3, 128, 128), bf16), ((ROWS, 128), f32), ((ROWS, 128), f32),
        ((2, ROWS, 128), bf16), ((80, ROWS), bf16), ((2, ROWS, CHUNK), f32), ((ROWS, 128), f32),
        ((ROWS, F), f32), ((ROWS, F), f32),
        ((DEPTH, 128), f32), ((ROWS, 128), f32),
        ((ROWS, 128), f32),
        ((ROWS // 2, 128), bf16), ((ROWS // 2, 128), bf16), ((ROWS // 2, 128), bf16),
        ((4, ROWS // 2, 128), bf16),
    ]
    dma = pltpu.SemaphoreType.DMA
    grads, generated = pl.pallas_call(
        kernel,
        out_shape=(
            jax.ShapeDtypeStruct((1, DEPTH, F), f32),
            jax.ShapeDtypeStruct((C, ROWS), bf16),
        ),
        in_specs=[pl.BlockSpec(memory_space=pltpu.HBM)] * 8,
        out_specs=(vmem, vmem),
        scratch_shapes=[pltpu.VMEM(shape, kind) for shape, kind in scratch]
        + [dma((8,))]
        + [dma((3, SIDE)) for _ in range(4)]
        + [dma((1,)), dma((1,)), dma((1,)), dma((4,)), dma((11,)), dma((11,))]
        + [pltpu.SemaphoreType.REGULAR],
        compiler_params=pltpu.CompilerParams(
            collective_id=0, has_side_effects=True, vmem_limit_bytes=32 * 2**20
        ),
    )(
        *(
            pltpu.with_memory_space_constraint(array, pltpu.HBM)
            for array in (
                sn.T, sc.T, lv.reshape(ROWS // 128, 128), emb, tim, gain, blk,
                rdo.transpose(0, 2, 1),
            )
        )
    )
    return grads, generated.T


def solution(mesh):
    in_specs = (
        P("fsdp", None),
        P("fsdp", None),
        P("fsdp"),
        P("role", None, None),
        P("role", None),
        P("role", None),
        P("role", "fsdp", None),
        P("role", None, None),
    )
    out_specs = (P("role", "fsdp", None), P("fsdp", None))
    return jax.shard_map(shards, mesh=mesh, in_specs=in_specs, out_specs=out_specs, check_vma=False)
```

time: 59.6 us -> 56 us (0.940)
  Pallas kernels: 57.5 us -> 53.9 us
    pallas_call x1, Pallas kernels: 57.5 us -> 53.9 us  [shards(): pl.pallas_call(kernel, out_shape=(jax.ShapeDtypeStruct((1, DEPTH, F), f32...]
where the time goes in v5:
time: 56 us; the launch traced here: 55.9 us
  Pallas kernels  53.9 us (96%)
  local copies, waits for them, and re-layouts  1.34 us (2%)
  between operations  0.64 us (1%)
    pallas_call x1, Pallas kernels, shards(): pl.pallas_call(kernel, out_shape=(jax.ShapeDtypeStruct((1, DEPTH, F), f32...  53.9 us
    unnamed x2, local copies, waits for them, and re-layouts  1.34 us

profile of v5, /device:TPU:2, one launch (start us, length us, event | category | flops | bytes accessed | tf_op | source)
XLA Modules:
  0.0 55.9 jit_solution(4676454599865627421)
XLA Ops:
  0.6 53.9 %shard_map.95 = (f32[1,48,1536]{2,1,0:T(8,128)S(1)}, bf16[64,384]{1,0:T(8,128)(2,1)S(1)}) custom-call(bf16[64,384]{1,0:T(8,128)(2,1)} %bitcast.7, bf16[64,384]{1,0:T(8,128)(2,1)} %bitcast.8, f32[3,128]{1,0:T(4,128)} %bitcast.9, bf16[1,64,3072]{2,1,0:T(8,128)(2,1)} %refs_3_.1, f32[1,3072]{1,0:T(1,128)} %refs_4_.1, f32[1,3072]{1,0:T(1,128)} %refs_5_.1, ...), custom_call_target="tpu_custom_call" | custom-call | tf_op jit(solution)/shard_map/pallas_call | solution.py:534
  54.5 0.7 %copy.12 = f32[1,48,1536]{2,1,0:T(8,128)} copy(f32[1,48,1536]{2,1,0:T(8,128)S(1)} %get-tuple-element.8) | data formatting | bytes 589824
  55.3 0.6 %copy.13 = bf16[384,64]{0,1:T(8,128)(2,1)} copy(bf16[384,64]{0,1:T(8,128)(2,1)S(1)} %bitcast.5) | data formatting | bytes 98304

commit v6 on v5

--- a/solution.py
+++ b/solution.py
@@ -74,7 +74,7 @@
 def step(
     hbm, fetch, grads, gen_out,
     sn, sc, lv, emb, tim, gain, blk, rdo, x_ref, vt, vrow, s_a, d_a, s_b, d_b, m_all, rsum, gen_f, rd_in, rs_row, rs_in,
-    t_a, e_a, t_b, e_b, h_buf,
+    t_a, e_a, t_b, e_b, e_c, h_buf,
     r2_all, gram, level, z_f32, z_all, z_t, rs_all, y_ref, hid, slope, lt, cot,
     noise_in, gen_pk, gen_in, out_pk, col_in,
     send_m, recv_m, send_h, recv_h, send_g, recv_g, send_c, recv_c, send_x, recv_x, turn,
@@ -317,13 +317,13 @@
     summed = total(summed, d_b)
     m_all[(slot, *own_block)] = summed[:, :HALF].astype(bf16)
     m_c = dict(zip(YX_ORDER, stage_c(m_all.at[slot], send_m, recv_m)))
-    for k in YX_ORDER:
-        m_c[k].start()
-
-        @pl.when(role == 0)
-        def _():
+
+    @pl.when(role == 0)
+    def _():
+        for k in YX_ORDER:
             x_matrix[k].start()
 
+    start(m_c.values())
     put_row(summed[:, HALF : HALF + 128] + summed[:, HALF + 128 :])
     v_full = vrow[0:1, :]
     v_high = v_full.astype(bf16).astype(f32)
@@ -360,7 +360,7 @@
         left = own_left if c < CHUNKS // 2 else other_left
         return pl.ds(pl.multiple_of(left + c % (CHUNKS // 2) * CHUNK, CHUNK), CHUNK)
 
-    def forward(net, critic, before=None):
+    def forward(net, critic, before=None, slopes_too=False):
         out = jnp.zeros((ROWS, 128), f32)
         through = jnp.zeros((ROWS, 128), f32)
         for c in range(CHUNKS):
@@ -370,11 +370,12 @@
             hidden = dot(z_all[net], m_all[net, :, cs]) * rs_all[net]
             square, half, value = gelu_parts(hidden)
             out += dot(value.astype(bf16), r2_all[net, cs, :])
-            if critic:
+            if critic or slopes_too:
                 rise = gelu_slope(square, half, value)
                 slope[:, cs] = rise * rs_all[net]
+            if critic:
                 through += dot_nt((rise * rsum[0:1, cs]).astype(bf16), m_all[net, :, cs])
-            else:
+            if not (critic or slopes_too):
                 hid[:, cs] = hidden
         return out.astype(bf16).astype(f32), through
 
@@ -410,7 +411,6 @@
 
     @pl.when(role == 0)
     def _():
-        gen_out[...] = gen_f[...].T[:C].astype(bf16)
         slopes()
         rows_turned()
         finish(x_matrix.values())
@@ -443,17 +443,15 @@
 
         @pl.when(role != 3)
         def _():
-            out, unused = forward(1, False)
+            out, unused = forward(1, False, None, True)
             out_pk[...] = pack(out).astype(bf16)
             to_gen(role, 0).start()
             cot[...] = out - gen_f[...]
 
-        @pl.when(role == 2)
+        @pl.when(role != 1)
         def _():
-            slopes()
-
-        rows_turned()
-        gen_out[...] = gen_f[...].T[:C].astype(bf16)
+            rows_turned()
+
         to_gen(role, 0).wait_send()
 
     finish(m_a)
@@ -462,6 +460,7 @@
 
     @pl.when(role == 1)
     def _():
+        gen_out[...] = gen_f[...].T[:C].astype(bf16)
         grads[...] = jnp.zeros_like(grads)
 
     @pl.when(role == 0)
@@ -480,34 +479,69 @@
         full = cot[...]
         c_high = full.astype(bf16).astype(f32)
         cot2 = jnp.where(lane < C, c_high, full - c_high).astype(bf16)
-        for c in range(CHUNKS):
-            cs = pl.ds(c * CHUNK, CHUNK)
-            hcot = (dot_nt(cot2, r2_all[slot, cs, :]) * slope[:, cs]).astype(bf16)
-            x_ref[:, cs] = dot(z_t[...], hcot)
-        x_ref[C : C + 1, :] = x_ref[C : C + 1, :] + x_ref[C + 1 : C + 2, :]
-        stage_a_fill(t_a, False)
-        h_a = stage_a(t_a, e_a, send_h, recv_h)
-        start(h_a)
-        arrive(h_a)
+        h_a = {copy_k: copy for copy_k, copy in zip(YX_ORDER, stage_a(t_a, e_a, send_h, recv_h))}
+
+        def row_tile(value):
+            value_high = value.astype(bf16).astype(f32)
+            return jnp.concatenate([value_high, value - value_high], axis=0).astype(bf16)
+
+        def half_out(left, offsets):
+            for c in range(CHUNKS // 2):
+                cs = pl.ds(pl.multiple_of(left + c * CHUNK, CHUNK), CHUNK)
+                hcot = (dot_nt(cot2, r2_all[slot, cs, :]) * slope[:, cs]).astype(bf16)
+                x_ref[:, cs] = dot(z_t[...], hcot)
+            for i in range(HALF // 128):
+                here = pl.ds(pl.multiple_of(left + i * 128, 128), 128)
+                vt[i : i + 1, :] = x_ref[C : C + 1, here] + x_ref[C + 1 : C + 2, here]
+            tile = row_tile(vt[0:8, :])
+            for k in offsets:
+                piece = lax.rem(p + k, SIDE)
+                top = pl.multiple_of(piece // 2 * 16, 16)
+                t_a[piece, :, :HALF] = x_ref[pl.ds(top, 16), pl.ds(left, HALF)].astype(bf16)
+                t_a[piece, :, HALF:] = tile
+                if k:
+                    h_a[k].start()
+
+        vt[...] = jnp.zeros_like(vt)
+        half_out(other_left, (5, 3, 7, 1))
+        half_out(own_left, (4, 2, 6, 0))
+        gen_out[...] = gen_f[...].T[:C].astype(bf16)
+        left = lt[...] * (1.0 / math.sqrt(ROWS * SIDE * SIDE))
+        l_high, l_low = split(left[:, :C])
+        arrive(h_a.values())
         summed = total(t_a[p], e_a)
-        t_b[...] = summed.astype(bf16)
+        t_b[:, :HALF] = summed[:, :HALF].astype(bf16)
+        t_b[:, HALF:] = row_tile(summed[0:8, HALF:] + summed[8:16, HALF:])
         h_b = stage_b(t_b, e_b, send_h, recv_h)
         start(h_b)
         arrive(h_b)
         summed = total(summed, e_b)
-        h_buf[pl.ds(own_top, 16), pl.ds(own_left, HALF)] = summed[:, :HALF].astype(bf16)
-        h_c = stage_c(h_buf, send_h, recv_h)
-        start(h_c)
-        put_row(summed[:, HALF:])
-        left = lt[...] * (1.0 / math.sqrt(ROWS * SIDE * SIDE))
-        l_high, l_low = split(left[:, :C])
-        base = left[:, C : C + 1] * vrow[0:1, :]
-        arrive(h_c)
+        e_c[0, :, :HALF] = summed[:, :HALF].astype(bf16)
+        e_c[0, :, HALF:] = row_tile(summed[0:8, HALF:] + summed[8:16, HALF:])
+        h_c = {
+            k: remote(e_c.at[0], e_c.at[k], send_h.at[2, k], recv_h.at[2, k], yx_peer(k))
+            for k in YX_ORDER
+        }
+        start(h_c.values())
+        for k in (0, 6, 2, 4, 1, 7, 3, 5):
+            if k:
+                h_c[k].wait_recv()
+            piece = lax.rem(p + SIDE - k, SIDE)
+            block = pl.ds(pl.multiple_of(lax.rem(piece, 2) * HALF, 128), HALF)
+            h_buf[pl.ds(pl.multiple_of(piece // 2 * 16, 16), 16), block] = e_c[k, :, :HALF]
+            if k < 2:
+                tile = e_c[k, :, HALF:].astype(f32)
+                vt[0:8, :] = tile[0:8] + tile[8:16]
+                for i in range(HALF // 128):
+                    here = pl.ds(
+                        pl.multiple_of((own_left if k == 0 else other_left) + i * 128, 128), 128
+                    )
+                    vrow[0:1, here] = vt[i : i + 1, :]
         full_h = h_buf[...]
-        grads[0] = base + dot(l_high, full_h) + dot(l_low, full_h)
-        finish(h_a)
+        grads[0] = left[:, C : C + 1] * vrow[0:1, :] + dot(l_high, full_h) + dot(l_low, full_h)
+        finish(h_a.values())
         finish(h_b)
-        finish(h_c)
+        finish(h_c.values())
 
 
 def shards(sn, sc, lv, emb, tim, gain, blk, rdo):
@@ -521,7 +555,8 @@
         ((2, 128, F), bf16), ((8, F), f32), ((ROWS, 128), f32),
         ((C, F), bf16), ((8, ROWS), f32), ((8, ROWS), f32),
         ((SIDE, 16, HALF + 128), bf16), ((SIDE, 16, HALF + 128), bf16),
-        ((16, HALF + 128), bf16), ((SIDE, 16, HALF + 128), bf16), ((C, F), bf16),
+        ((16, HALF + 128), bf16), ((SIDE, 16, HALF + 128), bf16),
+        ((SIDE, 16, HALF + 128), bf16), ((C, F), bf16),
         ((2, F, 128), bf16), ((3, 128, 128), bf16), ((ROWS, 128), f32), ((ROWS, 128), f32),
         ((2, ROWS, 128), bf16), ((80, ROWS), bf16), ((2, ROWS, CHUNK), f32), ((ROWS, 128), f32),
         ((ROWS, F), f32), ((ROWS, F), f32),

time: 56 us -> 55 us (0.982)
  Pallas kernels: 53.9 us -> 52.8 us
    pallas_call x1, Pallas kernels: 53.9 us -> 52.8 us  [shards(): pl.pallas_call(kernel, out_shape=(jax.ShapeDtypeStruct((1, DEPTH, F), f32...]
where the time goes in v6:
time: 55 us; the launch traced here: 54.8 us
  Pallas kernels  52.8 us (96%)
  local copies, waits for them, and re-layouts  1.34 us (2%)
  between operations  0.64 us (1%)
    pallas_call x1, Pallas kernels, shards(): pl.pallas_call(kernel, out_shape=(jax.ShapeDtypeStruct((1, DEPTH, F), f32...  52.8 us
    unnamed x2, local copies, waits for them, and re-layouts  1.34 us

profile of v6, /device:TPU:2, one launch (start us, length us, event | category | flops | bytes accessed | tf_op | source)
XLA Modules:
  0.0 54.8 jit_solution(17855635897649138768)
XLA Ops:
  0.6 52.8 %shard_map.95 = (f32[1,48,1536]{2,1,0:T(8,128)S(1)}, bf16[64,384]{1,0:T(8,128)(2,1)S(1)}) custom-call(bf16[64,384]{1,0:T(8,128)(2,1)} %bitcast.7, bf16[64,384]{1,0:T(8,128)(2,1)} %bitcast.8, f32[3,128]{1,0:T(4,128)} %bitcast.9, bf16[1,64,3072]{2,1,0:T(8,128)(2,1)} %refs_3_.1, f32[1,3072]{1,0:T(1,128)} %refs_4_.1, f32[1,3072]{1,0:T(1,128)} %refs_5_.1, ...), custom_call_target="tpu_custom_call" | custom-call | tf_op jit(solution)/shard_map/pallas_call | solution.py:569
  53.4 0.7 %copy.12 = f32[1,48,1536]{2,1,0:T(8,128)} copy(f32[1,48,1536]{2,1,0:T(8,128)S(1)} %get-tuple-element.8) | data formatting | bytes 589824
  54.2 0.6 %copy.13 = bf16[384,64]{0,1:T(8,128)(2,1)} copy(bf16[384,64]{0,1:T(8,128)(2,1)S(1)} %bitcast.5) | data formatting | bytes 98304

commit v7 on v6

--- a/solution.py
+++ b/solution.py
@@ -54,6 +54,11 @@
     return jnp.concatenate([jnp.where(left, value, turned), jnp.where(left, turned, value)], axis=0)
 
 
+def row_tile(value):
+    value_high = value.astype(bf16).astype(f32)
+    return jnp.concatenate([value_high, value - value_high], axis=0).astype(bf16)
+
+
 def gelu_parts(hidden):
     square = hidden * hidden
     half = 0.5 + 0.5 * jnp.tanh(hidden * (ROOT + CUBE * square))
@@ -73,7 +78,7 @@
 
 def step(
     hbm, fetch, grads, gen_out,
-    sn, sc, lv, emb, tim, gain, blk, rdo, x_ref, vt, vrow, s_a, d_a, s_b, d_b, m_all, rsum, gen_f, rd_in, rs_row, rs_in,
+    sn, sc, lv, emb, tim, gain, blk, rdo, x_ref, vt, vrow, s_a, d_a, s_b, d_b, m_all, tiles, rsum, gen_f, rd_in, rs_row, rs_in,
     t_a, e_a, t_b, e_b, e_c, h_buf,
     r2_all, gram, level, z_f32, z_all, z_t, rs_all, y_ref, hid, slope, lt, cot,
     noise_in, gen_pk, gen_in, out_pk, col_in,
@@ -134,18 +139,18 @@
     block = blk[0]
     x_ref[...] = dot(high, block) + dot(low, block)
 
-    def stage_a_fill(send, low_too):
+    def stage_a_fill(send):
         vt[...] = jnp.zeros_like(vt)
-        for i in range(F // 128):
-            vt[i : i + 1, :] = x_ref[C : C + 1, i * 128 : i * 128 + 128]
-        tile = vt[...]
-        for piece in range(SIDE):
-            top, left = piece // 2 * 16, piece % 2 * HALF
-            send[piece, :, :HALF] = x_ref[top : top + 16, left : left + HALF].astype(bf16)
-            v_high, v_low = split(tile)
-            send[piece, :, HALF : HALF + 128] = v_high
-            if low_too:
-                send[piece, :, HALF + 128 :] = v_low
+        for side in range(2):
+            for i in range(HALF // 128):
+                here = slice(side * HALF + i * 128, side * HALF + i * 128 + 128)
+                vt[i : i + 1, :] = x_ref[C : C + 1, here]
+            tile = row_tile(vt[0:8, :])
+            for piece in range(side, SIDE, 2):
+                top = piece // 2 * 16
+                part = x_ref[top : top + 16, side * HALF : side * HALF + HALF]
+                send[piece, :, :HALF] = part.astype(bf16)
+                send[piece, :, HALF:] = tile
 
     def stage_a(send, dest, ss, rr):
         return [
@@ -181,17 +186,12 @@
             copy.wait_send()
 
     def total(first, dest):
-        value = first.astype(f32)
-        for k in range(1, SIDE):
-            value = value + dest[k].astype(f32)
-        return value
-
-    def put_row(tile):
-        vt[...] = tile
-        for i in range(F // 128):
-            vrow[0:1, i * 128 : i * 128 + 128] = vt[i : i + 1, :]
-
-    stage_a_fill(s_a, True)
+        values = [first.astype(f32)] + [dest[k].astype(f32) for k in range(1, SIDE)]
+        while len(values) > 1:
+            values = [a + b for a, b in zip(values[::2], values[1::2])]
+        return values[0]
+
+    stage_a_fill(s_a)
     pl.semaphore_wait(barrier, 2 * (SIDE - 1) + 3)
     m_a = stage_a(s_a, d_a, send_m, recv_m)
 
@@ -265,8 +265,10 @@
     critic_here = (3, place)
     x_readout = remote(rdo.at[0], rd_in, send_x.at[8], recv_x.at[8], critic_here)
     x_scales = remote(rs_row, rs_in, send_x.at[9], recv_x.at[9], critic_here)
-    level_rows = m_all.at[0, pl.ds(C, 16), :]
-    x_level = remote(level_rows, level_rows, send_x.at[10], recv_x.at[10], critic_here)
+    beside = lax.rem(p + 1, SIDE) * SIDE + z
+    x_own = remote(tiles.at[0], tiles.at[2], send_x.at[10], recv_x.at[10], critic_here)
+    x_other = remote(tiles.at[0], tiles.at[3], send_x.at[11], recv_x.at[11], (3, beside))
+    x_tile = remote(tiles.at[0], tiles.at[1], send_x.at[12], recv_x.at[12], (role, beside))
     matrix_block = m_all.at[(0, *own_block)]
     x_matrix = {
         k: remote(
@@ -286,9 +288,7 @@
 
     summed = total(s_a[p], d_a)
     s_b[:, :HALF] = summed[:, :HALF].astype(bf16)
-    v_high, v_low = split(summed[:, HALF : HALF + 128] + summed[:, HALF + 128 :])
-    s_b[:, HALF : HALF + 128] = v_high
-    s_b[:, HALF + 128 :] = v_low
+    s_b[:, HALF:] = row_tile(summed[0:8, HALF:] + summed[8:16, HALF:])
     m_b = stage_b(s_b, d_b, send_m, recv_m)
     start(m_b)
 
@@ -324,18 +324,29 @@
             x_matrix[k].start()
 
     start(m_c.values())
-    put_row(summed[:, HALF : HALF + 128] + summed[:, HALF + 128 :])
-    v_full = vrow[0:1, :]
-    v_high = v_full.astype(bf16).astype(f32)
-    rows = lax.broadcasted_iota(jnp.int32, (16, F), 0)
-    m_all[slot, C : C + 16, :] = jnp.where(
-        (rows == 0) | (rows == 2), v_high, jnp.where(rows == 1, v_full - v_high, 0.0)
-    ).astype(bf16)
+    tiles[0] = row_tile(summed[0:8, HALF:] + summed[8:16, HALF:])
+    x_tile.start()
 
     @pl.when(role == 0)
     def _():
-        x_level.start()
+        x_own.start()
+        x_other.start()
         x_matrix[0].start()
+
+    def level_rows(net, left, tile):
+        rows = lax.broadcasted_iota(jnp.int32, (16, 128), 0)
+        value = tile.astype(f32)
+        for i in range(HALF // 128):
+            here = pl.ds(pl.multiple_of(left + i * 128, 128), 128)
+            m_all[net, C : C + 16, here] = jnp.where(
+                (rows == 0) | (rows == 2),
+                value[i : i + 1],
+                jnp.where(rows == 1, value[8 + i : 9 + i], 0.0),
+            ).astype(bf16)
+
+    level_rows(slot, own_left, tiles[0])
+    x_tile.wait_recv()
+    level_rows(slot, other_left, tiles[1])
 
     near, far = (2, 4, 6), (1, 3, 5, 7)
 
@@ -354,7 +365,10 @@
             scales = jnp.broadcast_to(rs_in[0:1, here], (128, 128)).T
             rs_all[0, here, :128] = scales
             rs_all[0, here, 128:] = scales
-        x_level.wait_recv()
+        x_own.wait_recv()
+        level_rows(0, own_left, tiles[2])
+        x_other.wait_recv()
+        level_rows(0, other_left, tiles[3])
 
     def columns(c):
         left = own_left if c < CHUNKS // 2 else other_left
@@ -414,7 +428,7 @@
         slopes()
         rows_turned()
         finish(x_matrix.values())
-        finish((x_readout, x_scales, x_level, hand_on))
+        finish((x_readout, x_scales, x_own, x_other, hand_on))
 
     @pl.when(role != 0)
     def _():
@@ -457,6 +471,7 @@
     finish(m_a)
     finish(m_b)
     finish(m_c.values())
+    x_tile.wait_send()
 
     @pl.when(role == 1)
     def _():
@@ -480,10 +495,6 @@
         c_high = full.astype(bf16).astype(f32)
         cot2 = jnp.where(lane < C, c_high, full - c_high).astype(bf16)
         h_a = {copy_k: copy for copy_k, copy in zip(YX_ORDER, stage_a(t_a, e_a, send_h, recv_h))}
-
-        def row_tile(value):
-            value_high = value.astype(bf16).astype(f32)
-            return jnp.concatenate([value_high, value - value_high], axis=0).astype(bf16)
 
         def half_out(left, offsets):
             for c in range(CHUNKS // 2):
@@ -550,9 +561,9 @@
         ((C, ROWS), bf16), ((C, ROWS), bf16), ((ROWS // 128, 128), f32), ((1, C, D), bf16),
         ((1, D), f32), ((1, D), f32), ((1, DEPTH, F), bf16), ((1, C, F), bf16),
         ((80, F), f32), ((16, 128), f32), ((8, F), f32),
-        ((SIDE, 16, HALF + 256), bf16), ((SIDE, 16, HALF + 256), bf16),
-        ((16, HALF + 256), bf16), ((SIDE, 16, HALF + 256), bf16),
-        ((2, 128, F), bf16), ((8, F), f32), ((ROWS, 128), f32),
+        ((SIDE, 16, HALF + 128), bf16), ((SIDE, 16, HALF + 128), bf16),
+        ((16, HALF + 128), bf16), ((SIDE, 16, HALF + 128), bf16),
+        ((2, 128, F), bf16), ((4, 16, 128), bf16), ((8, F), f32), ((ROWS, 128), f32),
         ((C, F), bf16), ((8, ROWS), f32), ((8, ROWS), f32),
         ((SIDE, 16, HALF + 128), bf16), ((SIDE, 16, HALF + 128), bf16),
         ((16, HALF + 128), bf16), ((SIDE, 16, HALF + 128), bf16),
@@ -577,7 +588,7 @@
         scratch_shapes=[pltpu.VMEM(shape, kind) for shape, kind in scratch]
         + [dma((8,))]
         + [dma((3, SIDE)) for _ in range(4)]
-        + [dma((1,)), dma((1,)), dma((1,)), dma((4,)), dma((11,)), dma((11,))]
+        + [dma((1,)), dma((1,)), dma((1,)), dma((4,)), dma((13,)), dma((13,))]
         + [pltpu.SemaphoreType.REGULAR],
         compiler_params=pltpu.CompilerParams(
             collective_id=0, has_side_effects=True, vmem_limit_bytes=32 * 2**20

time: 55 us -> 54.6 us (level)
  no operation moved by 1% of the time
where the time goes in v7:
time: 54.6 us; the launch traced here: 54.5 us
  Pallas kernels  52.5 us (96%)
  local copies, waits for them, and re-layouts  1.34 us (2%)
  between operations  0.64 us (1%)
    pallas_call x1, Pallas kernels, shards(): pl.pallas_call(kernel, out_shape=(jax.ShapeDtypeStruct((1, DEPTH, F), f32...  52.5 us
    unnamed x2, local copies, waits for them, and re-layouts  1.34 us

profile of v7, /device:TPU:2, one launch (start us, length us, event | category | flops | bytes accessed | tf_op | source)
XLA Modules:
  0.0 54.5 jit_solution(10293327725348124597)
XLA Ops:
  0.6 52.5 %shard_map.95 = (f32[1,48,1536]{2,1,0:T(8,128)S(1)}, bf16[64,384]{1,0:T(8,128)(2,1)S(1)}) custom-call(bf16[64,384]{1,0:T(8,128)(2,1)} %bitcast.7, bf16[64,384]{1,0:T(8,128)(2,1)} %bitcast.8, f32[3,128]{1,0:T(4,128)} %bitcast.9, bf16[1,64,3072]{2,1,0:T(8,128)(2,1)} %refs_3_.1, f32[1,3072]{1,0:T(1,128)} %refs_4_.1, f32[1,3072]{1,0:T(1,128)} %refs_5_.1, ...), custom_call_target="tpu_custom_call" | custom-call | tf_op jit(solution)/shard_map/pallas_call | solution.py:580
  53.1 0.7 %copy.12 = f32[1,48,1536]{2,1,0:T(8,128)} copy(f32[1,48,1536]{2,1,0:T(8,128)S(1)} %get-tuple-element.8) | data formatting | bytes 589824
  53.9 0.6 %copy.13 = bf16[384,64]{0,1:T(8,128)(2,1)} copy(bf16[384,64]{0,1:T(8,128)(2,1)S(1)} %bitcast.5) | data formatting | bytes 98304

commit v8 on v7

--- a/solution.py
+++ b/solution.py
@@ -16,7 +16,7 @@
 D = 3072
 F = 1536
 DEPTH = 48
-CHUNK = 256
+CHUNK = 768
 CHUNKS = F // CHUNK
 SIDE = 8
 HALF = F // 2
@@ -363,8 +363,7 @@
         for i in range(ROWS // 128):
             here = slice(i * 128, i * 128 + 128)
             scales = jnp.broadcast_to(rs_in[0:1, here], (128, 128)).T
-            rs_all[0, here, :128] = scales
-            rs_all[0, here, 128:] = scales
+            rs_all[0, here, :] = jnp.concatenate([scales] * (CHUNK // 128), axis=1)
         x_own.wait_recv()
         level_rows(0, own_left, tiles[2])
         x_other.wait_recv()

time: 54.6 us -> 53.9 us (0.987); the launches traced: 54.5 us -> 53 us
  Pallas kernels: 52.5 us -> 51 us
    pallas_call x1, Pallas kernels: 52.5 us -> 51 us  [shards(): pl.pallas_call(kernel, out_shape=(jax.ShapeDtypeStruct((1, DEPTH, F), f32...]
where the time goes in v8:
time: 53.9 us; the launch traced here: 53 us
  Pallas kernels  51 us (95%)
  local copies, waits for them, and re-layouts  1.34 us (2%)
  between operations  0.64 us (1%)
    pallas_call x1, Pallas kernels, shards(): pl.pallas_call(kernel, out_shape=(jax.ShapeDtypeStruct((1, DEPTH, F), f32...  51 us
    unnamed x2, local copies, waits for them, and re-layouts  1.34 us

profile of v8, /device:TPU:2, one launch (start us, length us, event | category | flops | bytes accessed | tf_op | source)
XLA Modules:
  0.0 53.0 jit_solution(18144946376792778920)
XLA Ops:
  0.6 51.0 %shard_map.95 = (f32[1,48,1536]{2,1,0:T(8,128)S(1)}, bf16[64,384]{1,0:T(8,128)(2,1)S(1)}) custom-call(bf16[64,384]{1,0:T(8,128)(2,1)} %bitcast.7, bf16[64,384]{1,0:T(8,128)(2,1)} %bitcast.8, f32[3,128]{1,0:T(4,128)} %bitcast.9, bf16[1,64,3072]{2,1,0:T(8,128)(2,1)} %refs_3_.1, f32[1,3072]{1,0:T(1,128)} %refs_4_.1, f32[1,3072]{1,0:T(1,128)} %refs_5_.1, ...), custom_call_target="tpu_custom_call" | custom-call | tf_op jit(solution)/shard_map/pallas_call | solution.py:579
  51.7 0.7 %copy.12 = f32[1,48,1536]{2,1,0:T(8,128)} copy(f32[1,48,1536]{2,1,0:T(8,128)S(1)} %get-tuple-element.8) | data formatting | bytes 589824
  52.4 0.6 %copy.13 = bf16[384,64]{0,1:T(8,128)(2,1)} copy(bf16[384,64]{0,1:T(8,128)(2,1)S(1)} %bitcast.5) | data formatting | bytes 98304
